TPU v7x, 32 devices: a whole 2x2x4 slice. The times are simulated.
32 devices in a mesh: box: 16 (over z, y, x), row: 2 (over core).
Axes of the slice: x: 2, y: 2, z: 4, core: 2. Of those that a mesh axis runs over, the one named last changes fastest.
Arguments:
- rhs: float32 [128, 64, 320], P('box'), may hold values from -6 to 6
- skel1: int32 [128, 192], P('box'), may hold values from 0 to 319, as said below
- red1: int32 [128, 128], P('box'), may hold values from 0 to 319, as said below
- interp1: bfloat16 [128, 128, 192], P('box', None, 'row'), may hold values from -0.5 to 0.5
- inv1: bfloat16 [128, 128, 128], P('box', None, 'row'), may hold values from -0.5 to 0.5
- couple1: bfloat16 [128, 8, 128, 192], P('box', None, None, 'row'), may hold values from -0.5 to 0.5
- near1: int32 [128, 8], P('box'), may hold values from -1 to 127, as said below
- skel2: int32 [16, 384], P('box'), may hold values from 0 to 1535, as said below
- red2: int32 [16, 1152], P('box'), may hold values from 0 to 1535, as said below
- interp2: bfloat16 [16, 1152, 384], P('box', None, 'row'), may hold values from -0.1875 to 0.1875
- inv2: bfloat16 [16, 1152, 1152], P('box', None, 'row'), may hold values from -0.1875 to 0.1875
- panel2: bfloat16 [16, 2, 1152, 384], P('box', None, None, 'row'), may hold values from -0.1875 to 0.1875
- near2: int32 [16, 2], P('box'), may hold values from -1 to 15, as said below
Outputs:
- red_one: float32 [128, 64, 128], P('box', None, 'row')
- red_two: float32 [16, 64, 1152], P('box', None, 'row')
- skel_two: float32 [16, 64, 384], P('box', None, 'row')
Inputs may be any that keep to these rules, and one draw needn't show every extreme that they name: For each leaf box, skel1 and red1 together hold every number below 320 exactly once. `red1`: see skel1. For each parent box, skel2 and red2 together hold every number below 1536 exactly once. `red2`: see skel2. `near1`: an entry of box b is -1 or another leaf box c with |c // 8 - b // 8| <= 2; a box may be named twice. `near2`: slot 0 of parent q is q - 1 or -1, slot 1 is q + 1 or -1.
All inputs are finite; a program needn't handle non-finite values.
Results may differ from a plain program's by a relative error of at most 0.0046.
Values may be sent and summed in bfloat16 or wider, within the bound.
No kernel may reach another device: no remote copies, remote signals or barrier semaphores. Data moves between devices by JAX's collectives and lax.ppermute only.
A program may use at most 64 MiB of HBM per device.

v0:
```python
import jax
import jax.numpy as jnp
from jax import lax
from jax.sharding import PartitionSpec as P


def shifted(block, axis, distance):
    devices = range(lax.axis_size(axis))
    route = [(i - distance, i) for i in devices if i - distance in devices]
    return lax.ppermute(block, axis, route)


def pick(values, index):
    return jax.vmap(lambda block, where: block[:, where])(values, index)


def route(updates, near, reach):
    groups = updates.shape[0]
    anchor = lax.axis_index("box")
    valid = near >= 0
    target = jnp.where(valid, near, 0)
    offset = target // groups - anchor
    slot = target % groups
    spots = jnp.arange(2 * reach + 1, dtype=jnp.int32) - reach
    places = jnp.arange(groups, dtype=jnp.int32)
    onehot = (
        valid[:, :, None, None]
        & (offset[:, :, None, None] == spots[None, None, :, None])
        & (slot[:, :, None, None] == places[None, None, None, :])
    ).astype(jnp.float32)
    outgoing = jnp.einsum("gnos,gnkc->oskc", onehot, updates, precision=lax.Precision.HIGHEST)
    total = outgoing[reach]
    for section in range(1, reach + 1):
        for sign in (1, -1):
            moved = shifted(outgoing[reach + sign * section], "box", sign * section)
            total = total + moved
    return total


def shards(
    rhs, skel1, red1, interp1, inv1, couple1, near1, skel2, red2, interp2, inv2, panel2, near2
):
    row_index = lax.axis_index("row")
    s1_block = interp1.shape[2]
    s2_block = interp2.shape[2]
    xr1 = pick(rhs, red1).astype(jnp.bfloat16)
    own_skel1 = lax.dynamic_slice_in_dim(skel1, row_index * s1_block, s1_block, 1)
    ys1 = pick(rhs, own_skel1) - jnp.einsum(
        "bkr,brs->bks", xr1, interp1, preferred_element_type=jnp.float32
    )
    red_one = jnp.einsum("bkr,brq->bkq", xr1, inv1, preferred_element_type=jnp.float32)
    w_one = red_one.astype(jnp.bfloat16)
    u_one = jnp.einsum(
        "bkr,bjrs->bjks",
        lax.all_gather(w_one, "row", axis=2, tiled=True),
        couple1,
        preferred_element_type=jnp.float32,
    )
    routed_one = route(u_one, near1, 2)
    own_full = lax.all_gather(ys1, "row", axis=2, tiled=True)
    added_full = lax.all_gather(routed_one, "row", axis=2, tiled=True)
    gathered = own_full + added_full
    children, columns, skeletons = gathered.shape
    parent = jnp.transpose(gathered, (1, 0, 2)).reshape(1, columns, children * skeletons)
    xr2 = pick(parent, red2).astype(jnp.bfloat16)
    own_skel2 = lax.dynamic_slice_in_dim(skel2, row_index * s2_block, s2_block, 1)
    ys2 = pick(parent, own_skel2) - jnp.einsum(
        "pkr,prs->pks", xr2, interp2, preferred_element_type=jnp.float32
    )
    red_two = jnp.einsum("pkr,prq->pkq", xr2, inv2, preferred_element_type=jnp.float32)
    u_two = jnp.einsum("kr,jrs->jks", xr2[0], panel2[0], preferred_element_type=jnp.float32)[None]
    routed_two = route(u_two, near2, 1)
    return (red_one, red_two, ys2 + routed_two)


def solution(mesh):
    return jax.shard_map(
        shards,
        mesh=mesh,
        in_specs=(
            P("box", None, None),
            P("box", None),
            P("box", None),
            P("box", None, "row"),
            P("box", None, "row"),
            P("box", None, None, "row"),
            P("box", None),
            P("box", None),
            P("box", None),
            P("box", None, "row"),
            P("box", None, "row"),
            P("box", None, None, "row"),
            P("box", None),
        ),
        out_specs=(P("box", None, "row"), P("box", None, "row"), P("box", None, "row")),
        check_vma=False,
    )
```

profile of v0, /device:TPU:24, one launch (start us, length us, event | category | flops | bytes accessed | tf_op | source)
XLA Modules:
  0.0 70.6 jit_solution(17534399115924622717)
XLA Ops:
  0.6 0.0 copy-start
  0.6 0.0 copy-start.7
  0.7 1.6 %copy.47 = f32[8,64,320]{1,2,0:T(8,128)S(1)} copy(f32[8,64,320]{2,1,0:T(8,128)} %param.13) | data formatting | bytes 1310720 | tf_op args[0]
  2.3 0.0 copy-done.7
  2.3 0.0 copy-start.4
  2.4 0.0 copy-start.5
  2.4 6.9 %gather_fusion = bf16[1024,64]{1,0:T(8,128)(2,1)S(1)} fusion(f32[8,64,320]{1,2,0:T(8,128)S(1)} %copy.47, s32[1024]{0:T(1024)S(1)} %fusion.40), kind=kCustom, calls=%fused_computation | custom fusion | bytes 270336 | tf_op jit(solution)/shard_map/vmap()/gather | solution.py:14
  9.3 0.0 copy-done.4
  9.3 1.0 %fusion.63 = (bf16[8,64,64]{2,1,0:T(8,128)(2,1)S(1)}, f32[8,64,64]{2,1,0:T(8,128)}) fusion(bf16[8,128,64]{2,1,0:T(8,128)(2,1)S(1)} %bitcast.109, bf16[8,128,64]{1,2,0:T(8,128)(2,1)S(1)} %copy-done.4), kind=kOutput, calls=%fused_computation.95 | convolution fusion | flops 8421376 | bytes 458752 | tf_op jit(solution)/shard_map/bkr,brq->bkq/dot_general | solution.py:51
  10.2 0.1 copy.54
  10.4 2.0 %all_gather.10 = bf16[8,64,128]{1,0,2:T(8,128)(2,1)S(1)} all-gather(bf16[8,64,64]{1,0,2:T(8,128)(2,1)S(1)} %copy.54), channel_id=1, replica_groups=mesh['box'=16,'row'=2] {'row'}, dimensions={2}, use_global_device_ids=true | all-gather | bytes 196608 | tf_op jit(solution)/shard_map/all_gather | solution.py:55
  12.4 0.0 copy-done.5
  12.4 0.0 copy-done
  12.4 1.3 %convolution_bitcast_fusion = f32[8,8,64,96]{3,2,1,0:T(8,128)S(1)} fusion(bf16[8,8,128,96]{2,3,1,0:T(8,128)(2,1)S(1)} %copy-done, bf16[8,64,128,1]{1,0,2,3:T(8,128)(2,1)S(1)} %bitcast.112), kind=kOutput, calls=%fused_computation.7 | convolution fusion | flops 100663296 | bytes 3276800 | tf_op jit(solution)/shard_map/bkr,bjrs->bjks/dot_general | solution.py:53
  13.7 0.1 compare_and_fusion
  13.7 3.2 %fusion.3 = f32[5,8,64,96]{3,1,2,0:T(8,128)S(1)} fusion(f32[8,8,64,96]{3,2,1,0:T(8,128)S(1)} %convolution_bitcast_fusion, pred[8,8,8]{1,2,0:T(8,128)(4,1)S(1)} %iota_compare_fusion, pred[8,8,5]{1,0,2:T(8,128)(4,1)S(1)} %compare_and_fusion), kind=kOutput, calls=%fused_computation.8 | convolution fusion | flops 188746240 | bytes 2556736 | tf_op jit(solution)/shard_map/gnos,gnkc->oskc/dot_general | solution.py:31
  17.0 1.1 %copy-done.2 = f32[5,8,64,96]{3,1,2,0:T(8,128)} copy-done((f32[5,8,64,96]{3,1,2,0:T(8,128)}, f32[5,8,64,96]{3,1,2,0:T(8,128)S(1)}, u32[]{:S(2)}) %copy-start.2) | copy-done | bytes 983064
  18.1 0.0 copy-start.8
  18.1 1.0 %slice_bitcast_fusion.3 = (f32[8,64,96]{2,0,1:T(8,128)}, f32[8,64,96]{2,0,1:T(8,128)}, f32[8,64,96]{2,0,1:T(8,128)}, f32[8,64,96]{2,0,1:T(8,128)}) fusion(f32[5,8,64,96]{3,1,2,0:T(8,128)S(1)} %fusion.3), kind=kLoop, calls=%fused_computation.23 | loop fusion | bytes 1572864 | tf_op jit(solution)/shard_map/squeeze | solution.py:35
  19.1 3.3 %collective-permute-start.3 = (f32[8,64,96]{2,0,1:T(8,128)}, f32[8,64,96]{2,0,1:T(8,128)}, u32[]{:S(2)}, u32[]{:S(2)}) collective-permute-start(f32[8,64,96]{2,0,1:T(8,128)} %get-tuple-element.4), channel_id=1, source_target_pairs={{4,0},{6,2},{8,4},{10,6},{12,8},{14,10},{16,12},{18,14},{20,16},{2... | collective-permute-start | bytes 589832 | tf_op jit(solution)/shard_map/ppermute | solution.py:10
  22.4 3.2 %collective-permute-start.2 = (f32[8,64,96]{2,0,1:T(8,128)}, f32[8,64,96]{2,0,1:T(8,128)}, u32[]{:S(2)}, u32[]{:S(2)}) collective-permute-start(f32[8,64,96]{2,0,1:T(8,128)} %get-tuple-element.5), channel_id=1, source_target_pairs={{0,4},{2,6},{4,8},{6,10},{8,12},{10,14},{12,16},{14,18},{16,20},{1... | collective-permute-start | bytes 589832 | tf_op jit(solution)/shard_map/ppermute | solution.py:10
  25.7 4.5 %collective-permute-start.1 = (f32[8,64,96]{2,0,1:T(8,128)}, f32[8,64,96]{2,0,1:T(8,128)}, u32[]{:S(2)}, u32[]{:S(2)}) collective-permute-start(f32[8,64,96]{2,0,1:T(8,128)} %get-tuple-element.6), channel_id=1, source_target_pairs={{2,0},{4,2},{6,4},{8,6},{10,8},{12,10},{14,12},{16,14},{18,16},{20... | collective-permute-start | bytes 589832 | tf_op jit(solution)/shard_map/ppermute | solution.py:10
  30.1 1.9 %collective-permute-start = (f32[8,64,96]{2,0,1:T(8,128)}, f32[8,64,96]{2,0,1:T(8,128)}, u32[]{:S(2)}, u32[]{:S(2)}) collective-permute-start(f32[8,64,96]{2,0,1:T(8,128)} %get-tuple-element.3), channel_id=1, source_target_pairs={{0,2},{2,4},{4,6},{6,8},{8,10},{10,12},{12,14},{14,16},{16,18},{18... | collective-permute-start | bytes 589832 | tf_op jit(solution)/shard_map/ppermute | solution.py:10
  32.1 0.0 copy-done.8
  32.1 0.1 fusion.44
  32.2 0.1 reshape.177
  32.2 5.2 %gather_fusion.1 = f32[768,64]{1,0:T(8,128)S(1)} fusion(f32[8,64,320]{1,2,0:T(8,128)S(1)} %copy.47, s32[768]{0:T(1024)S(1)} %reshape.177), kind=kCustom, calls=%fused_computation.1 | custom fusion | bytes 399360 | tf_op jit(solution)/shard_map/vmap()/gather | solution.py:14
  37.5 0.2 copy.51
  37.6 0.0 copy-start.6
  37.7 0.0 copy-start.10
  37.7 0.0 copy-start.9
  37.7 1.2 %convolution_subtract_fusion = f32[8,64,96]{2,1,0:T(8,128)S(1)} fusion(bf16[8,128,64]{2,1,0:T(8,128)(2,1)S(1)} %bitcast.110, bf16[8,128,96]{1,2,0:T(8,128)(2,1)} %param.16, f32[8,96,64]{1,2,0:T(8,128)S(1)} %copy.51), kind=kOutput, calls=%fused_computation.11 | convolution fusion | flops 12632064 | bytes 720896 | tf_op jit(solution)/shard_map/bkr,brs->bks/dot_general | solution.py:48
  38.9 0.2 copy.53
  39.1 2.4 %all_gather.9 = f32[8,64,192]{1,0,2:T(8,128)S(1)} all-gather(f32[8,64,96]{1,0,2:T(8,128)S(1)} %copy.53), channel_id=1, replica_groups=mesh['box'=16,'row'=2] {'row'}, dimensions={2}, use_global_device_ids=true | all-gather | bytes 589824 | tf_op jit(solution)/shard_map/all_gather | solution.py:60
  41.5 0.0 copy-done.6
  41.5 0.0 copy-done.10
  41.6 0.0 copy-done.9
  41.6 0.1 fusion.50
  41.7 0.0 collective-permute-done.3
  41.7 0.0 collective-permute-done.2
  41.7 0.0 collective-permute-done.1
  41.7 0.2 collective-permute-done
  41.9 1.3 %fusion.18 = f32[8,64,96]{2,0,1:T(8,128)S(1)} fusion(f32[8,64,96]{2,0,1:T(8,128)} %collective-permute-done.3, f32[8,64,96]{2,0,1:T(8,128)} %collective-permute-done.2, f32[8,64,96]{2,0,1:T(8,128)} %collective-permute-done.1, f32[8,64,96]{2,0,1:T(8,128)} %collective-permute-done, f32[5,8,64,96]{3,1,2,0:T(8,128)} %copy-done.2), kind=kLoop, calls=%fused_computation.28 | loop fusion | flops 196608 | bytes 1179648 | tf_op jit(solution)/shard_map/add | solution.py:36
  43.2 0.2 copy.57
  43.4 2.4 %all_gather.11 = f32[8,64,192]{1,0,2:T(8,128)S(1)} all-gather(f32[8,64,96]{1,0,2:T(8,128)S(1)} %copy.57), channel_id=1, replica_groups=mesh['box'=16,'row'=2] {'row'}, dimensions={2}, use_global_device_ids=true | all-gather | bytes 589824 | tf_op jit(solution)/shard_map/all_gather | solution.py:61
  45.8 0.1 add_bitcast_fusion
  45.9 0.2 copy.78
  46.0 5.9 %gather_fusion.2 = bf16[1152,64]{1,0:T(8,128)(2,1)S(1)} fusion(f32[1,64,1536]{1,2,0:T(8,128)S(1)} %bitcast.107, s32[1152]{0:T(1024)S(1)} %fusion.34), kind=kCustom, calls=%fused_computation.2 | custom fusion | bytes 304128 | tf_op jit(solution)/shard_map/vmap()/gather | solution.py:14
  52.0 0.0 copy-start.1
  52.0 1.7 %convolution_bitcast_fusion.1 = f32[2,64,192]{2,1,0:T(8,128)S(1)} fusion(bf16[1,2,1152,192]{2,3,1,0:T(8,128)(2,1)} %param.24, bf16[1152,64]{1,0:T(8,128)(2,1)S(1)} %gather_fusion.2), kind=kOutput, calls=%fused_computation.13 | convolution fusion | flops 56623104 | bytes 1130496 | tf_op jit(solution)/shard_map/kr,jrs->jks/dot_general | solution.py:71
  53.7 0.5 fusion.22
  54.3 0.1 fusion.62
  54.4 6.3 %collective-permute-start.5 = (f32[1,64,192]{2,1,0:T(8,128)S(1)}, f32[1,64,192]{2,1,0:T(8,128)S(1)}, u32[]{:S(2)}, u32[]{:S(2)}) collective-permute-start(f32[1,64,192]{2,1,0:T(8,128)S(1)} %copy.82), channel_id=1, source_target_pairs={{2,0},{4,2},{6,4},{8,6},{10,8},{12,10},{14,12},{16,14},{18,16},{20... | collective-permute-start | bytes 147464 | tf_op jit(solution)/shard_map/ppermute | solution.py:10
  60.7 0.6 copy.81
  61.4 0.0 copy-start.3
  61.4 2.0 %collective-permute-start.4 = (f32[1,64,192]{2,1,0:T(8,128)}, f32[1,64,192]{2,1,0:T(8,128)S(1)}, u32[]{:S(2)}, u32[]{:S(2)}) collective-permute-start(f32[1,64,192]{2,1,0:T(8,128)} %copy.81), channel_id=1, source_target_pairs={{0,2},{2,4},{4,6},{6,8},{8,10},{10,12},{12,14},{14,16},{16,18},{18... | collective-permute-start | bytes 147464 | tf_op jit(solution)/shard_map/ppermute | solution.py:10
  63.4 0.0 copy-done.1
  63.4 1.2 %fusion.8 = f32[1,64,576]{2,1,0:T(8,128)} fusion(bf16[1,1152,576]{1,2,0:T(8,128)(2,1)S(1)} %copy-done.1, bf16[1152,64]{1,0:T(8,128)(2,1)S(1)} %gather_fusion.2), kind=kOutput, calls=%fused_computation.12 | convolution fusion | flops 84934656 | bytes 1622016 | tf_op jit(solution)/shard_map/pkr,prq->pkq/dot_general | solution.py:70
  64.6 1.6 %gather_fusion.3 = f32[192,64]{1,0:T(8,128)S(1)} fusion(f32[1,64,1536]{1,2,0:T(8,128)S(1)} %bitcast.108, s32[192]{0:T(256)S(1)} %bitcast.106), kind=kCustom, calls=%fused_computation.3 | custom fusion | bytes 99840 | tf_op jit(solution)/shard_map/vmap()/gather | solution.py:14
  66.3 0.1 copy.61
  66.4 0.0 collective-permute-done.5
  66.4 3.3 %collective-permute-done.4 = f32[1,64,192]{2,1,0:T(8,128)S(1)} collective-permute-done((f32[1,64,192]{2,1,0:T(8,128)}, f32[1,64,192]{2,1,0:T(8,128)S(1)}, u32[]{:S(2)}, u32[]{:S(2)}) %collective-permute-start.4) | collective-permute-done | bytes 49184 | tf_op jit(solution)/shard_map/ppermute | solution.py:10
  69.7 0.0 copy-done.3
  69.7 0.9 %fusion.27 = f32[1,64,192]{2,1,0:T(8,128)} fusion(f32[1,64,192]{2,1,0:T(8,128)S(1)} %collective-permute-done.5, f32[1,64,192]{2,1,0:T(8,128)S(1)} %collective-permute-done.4, f32[1,64,192]{2,0,1:T(1,128)S(1)} %get-tuple-element.7, bf16[1,1152,192]{1,2,0:T(8,128)(2,1)S(1)} %copy-done.3, f32[192,64]{0,1:T(8,128)S(1)} %copy.61, ...), kind=kOutput, calls=%fused_computation.38 | convolution fusion | flops 28360704 | bytes 835584 | tf_op jit(solution)/shard_map/pkr,prs->pks/dot_general | solution.py:67
  (15 shorter events, 0.1 us)
Async XLA Ops:
  0.6 11.8 %copy-start = (bf16[8,8,128,96]{2,3,1,0:T(8,128)(2,1)S(1)}, bf16[8,8,128,96]{2,3,1,0:T(8,128)(2,1)}, u32[]{:S(2)}) copy-start(bf16[8,8,128,96]{2,3,1,0:T(8,128)(2,1)} %param.18) | copy-start | bytes 4718596
  0.6 1.7 %copy-start.7 = (s32[8,128]{1,0:T(8,128)S(1)}, s32[8,128]{1,0:T(8,128)}, u32[]{:S(2)}) copy-start(s32[8,128]{1,0:T(8,128)} %param.15) | copy-start | bytes 12292
  2.3 6.9 %copy-start.4 = (bf16[8,128,64]{1,2,0:T(8,128)(2,1)S(1)}, bf16[8,128,64]{1,2,0:T(8,128)(2,1)}, u32[]{:S(2)}) copy-start(bf16[8,128,64]{1,2,0:T(8,128)(2,1)} %param.17) | copy-start | bytes 393220
  2.4 10.0 %copy-start.5 = (s32[8,8]{1,0:T(8,128)S(1)}, s32[8,8]{1,0:T(8,128)}, u32[]{:S(2)}) copy-start(s32[8,8]{1,0:T(8,128)} %param.19) | copy-start | bytes 772
  17.0 1.1 %copy-start.2 = (f32[5,8,64,96]{3,1,2,0:T(8,128)}, f32[5,8,64,96]{3,1,2,0:T(8,128)S(1)}, u32[]{:S(2)}) copy-start(f32[5,8,64,96]{3,1,2,0:T(8,128)S(1)} %fusion.3) | copy-start | bytes 2949124
  18.1 14.0 %copy-start.8 = (s32[8,192]{1,0:T(8,128)S(1)}, s32[8,192]{1,0:T(8,128)}, u32[]{:S(2)}) copy-start(s32[8,192]{1,0:T(8,128)} %param.14) | copy-start | bytes 18436
  19.1 22.6 %collective-permute-start.3 = (f32[8,64,96]{2,0,1:T(8,128)}, f32[8,64,96]{2,0,1:T(8,128)}, u32[]{:S(2)}, u32[]{:S(2)}) collective-permute-start(f32[8,64,96]{2,0,1:T(8,128)} %get-tuple-element.4), channel_id=1, source_target_pairs={{4,0},{6,2},{8,4},{10,6},{12,8},{14,10},{16,12},{18,14},{20,16},{2... | collective-permute-start | bytes 589832 | tf_op jit(solution)/shard_map/ppermute | solution.py:10
  22.4 19.3 %collective-permute-start.2 = (f32[8,64,96]{2,0,1:T(8,128)}, f32[8,64,96]{2,0,1:T(8,128)}, u32[]{:S(2)}, u32[]{:S(2)}) collective-permute-start(f32[8,64,96]{2,0,1:T(8,128)} %get-tuple-element.5), channel_id=1, source_target_pairs={{0,4},{2,6},{4,8},{6,10},{8,12},{10,14},{12,16},{14,18},{16,20},{1... | collective-permute-start | bytes 589832 | tf_op jit(solution)/shard_map/ppermute | solution.py:10
  25.7 16.1 %collective-permute-start.1 = (f32[8,64,96]{2,0,1:T(8,128)}, f32[8,64,96]{2,0,1:T(8,128)}, u32[]{:S(2)}, u32[]{:S(2)}) collective-permute-start(f32[8,64,96]{2,0,1:T(8,128)} %get-tuple-element.6), channel_id=1, source_target_pairs={{2,0},{4,2},{6,4},{8,6},{10,8},{12,10},{14,12},{16,14},{18,16},{20... | collective-permute-start | bytes 589832 | tf_op jit(solution)/shard_map/ppermute | solution.py:10
  30.1 11.8 %collective-permute-start = (f32[8,64,96]{2,0,1:T(8,128)}, f32[8,64,96]{2,0,1:T(8,128)}, u32[]{:S(2)}, u32[]{:S(2)}) collective-permute-start(f32[8,64,96]{2,0,1:T(8,128)} %get-tuple-element.3), channel_id=1, source_target_pairs={{0,2},{2,4},{4,6},{6,8},{8,10},{10,12},{12,14},{14,16},{16,18},{18... | collective-permute-start | bytes 589832 | tf_op jit(solution)/shard_map/ppermute | solution.py:10
  37.6 3.8 %copy-start.6 = (s32[1,1152]{1,0:T(1,128)S(1)}, s32[1,1152]{1,0:T(1,128)}, u32[]{:S(2)}) copy-start(s32[1,1152]{1,0:T(1,128)} %param.21) | copy-start | bytes 13828
  37.7 3.9 %copy-start.10 = (s32[1,2]{1,0:T(1,128)S(1)}, s32[1,2]{1,0:T(1,128)}, u32[]{:S(2)}) copy-start(s32[1,2]{1,0:T(1,128)} %param.25) | copy-start | bytes 28
  37.7 3.9 %copy-start.9 = (s32[1,384]{1,0:T(1,128)S(1)}, s32[1,384]{1,0:T(1,128)}, u32[]{:S(2)}) copy-start(s32[1,384]{1,0:T(1,128)} %param.20) | copy-start | bytes 4612
  52.0 11.4 %copy-start.1 = (bf16[1,1152,576]{1,2,0:T(8,128)(2,1)S(1)}, bf16[1,1152,576]{1,2,0:T(8,128)(2,1)}, u32[]{:S(2)}) copy-start(bf16[1,1152,576]{1,2,0:T(8,128)(2,1)} %param.23) | copy-start | bytes 3981316
  54.4 11.9 %collective-permute-start.5 = (f32[1,64,192]{2,1,0:T(8,128)S(1)}, f32[1,64,192]{2,1,0:T(8,128)S(1)}, u32[]{:S(2)}, u32[]{:S(2)}) collective-permute-start(f32[1,64,192]{2,1,0:T(8,128)S(1)} %copy.82), channel_id=1, source_target_pairs={{2,0},{4,2},{6,4},{8,6},{10,8},{12,10},{14,12},{16,14},{18,16},{20... | collective-permute-start | bytes 147464 | tf_op jit(solution)/shard_map/ppermute | solution.py:10
  61.4 8.3 %copy-start.3 = (bf16[1,1152,192]{1,2,0:T(8,128)(2,1)S(1)}, bf16[1,1152,192]{1,2,0:T(8,128)(2,1)}, u32[]{:S(2)}) copy-start(bf16[1,1152,192]{1,2,0:T(8,128)(2,1)} %param.22) | copy-start | bytes 1327108
  61.4 8.3 %collective-permute-start.4 = (f32[1,64,192]{2,1,0:T(8,128)}, f32[1,64,192]{2,1,0:T(8,128)S(1)}, u32[]{:S(2)}, u32[]{:S(2)}) collective-permute-start(f32[1,64,192]{2,1,0:T(8,128)} %copy.81), channel_id=1, source_target_pairs={{0,2},{2,4},{4,6},{6,8},{8,10},{10,12},{12,14},{14,16},{16,18},{18... | collective-permute-start | bytes 147464 | tf_op jit(solution)/shard_map/ppermute | solution.py:10
where the time goes:
time: 71 us; the launch traced here: 70.6 us
  local copies, waits for them, and re-layouts  25.3 us (36%)
  starting transfers between devices  21.2 us (30%)
  matrix products  11.1 us (16%)
  blocking collectives  6.73 us (9%)
  waiting for transfers between devices  3.48 us (5%)
  other arithmetic  1.75 us (2%)
  between operations  1.03 us (1%)
    ppermute x6, starting transfers between devices, shifted(): return lax.ppermute(block, axis, route)  21.2 us
    gather x9, local copies, waits for them, and re-layouts, pick(): return jax.vmap(lambda block, where: block[:, where])(values, index)  20 us
    dot_general x2, matrix products, route(): jnp.einsum('gnos,gnkc->oskc', onehot, updates, precision=lax.Precision.HI...  3.78 us
    ppermute x6, waiting for transfers between devices, shifted(): return lax.ppermute(block, axis, route)  3.48 us
    unnamed x25, local copies, waits for them, and re-layouts  3.44 us
    all_gather x1, blocking collectives, shards(): added_full = lax.all_gather(routed_one, 'row', axis=2, tiled=True)  2.37 us
    all_gather x1, blocking collectives, shards(): own_full = lax.all_gather(ys1, 'row', axis=2, tiled=True)  2.37 us
    all_gather x1, blocking collectives, shards(): lax.all_gather(w_one, 'row', axis=2, tiled=True)  1.99 us
  transfers between devices with their start and end apart: 6, of which 2 were waited for; matrix products, arithmetic and copies ran while one was open for 15% of the time, Pallas kernels for 0%

commit v1 on v0

v1 whole, which is shorter than its diff:
```python
import functools

import jax
import jax.numpy as jnp
from jax import lax
from jax.experimental import pallas as pl
from jax.experimental.pallas import tpu as pltpu
from jax.sharding import PartitionSpec as P

F32 = jnp.float32
BF16 = jnp.bfloat16
REACH = 2


def row_pieces(block):
    rows = lax.axis_size("row")
    others = [
        lax.ppermute(block, "row", [(i, i ^ t) for i in range(rows)]) for t in range(1, rows)
    ]
    return [block] + others


def box_permute(block, distance, flip):
    boxes, rows = lax.axis_size("box"), lax.axis_size("row")
    route = []
    for box in range(boxes):
        for row in range(rows):
            target = box + (distance if (row % 2 == 0) != flip else -distance)
            inside = 0 <= target < boxes
            place = target * rows + row if inside else box * rows + (row ^ 1)
            route.append((box * rows + row, place))
    return lax.ppermute(block, ("box", "row"), route)


def onehot(index, count, dtype=BF16):
    spots = lax.broadcasted_iota(jnp.int32, (count, index.shape[1]), 0)
    return jnp.where(spots == index, 1.0, 0.0).astype(dtype)


def dot(a, b):
    return jnp.dot(a, b, preferred_element_type=F32)


def dot_t(a, b):
    return lax.dot_general(a, b, (((1,), (1,)), ((), ())), preferred_element_type=F32)


def turned(panel):
    return jnp.swapaxes(panel, -1, -2)


def own_part(values, block):
    row = lax.axis_index("row")
    chosen = values[:, :block]
    for place in range(1, values.shape[1] // block):
        part = values[:, place * block : (place + 1) * block]
        chosen = jnp.where(row == place, part, chosen)
    return chosen


def call(body, out_shape, scratch=(), vmem=48 << 20, flops=0, size=0):
    return pl.pallas_call(
        body,
        out_shape=out_shape,
        scratch_shapes=list(scratch),
        compiler_params=pltpu.CompilerParams(vmem_limit_bytes=vmem),
        cost_estimate=pl.CostEstimate(flops=flops, bytes_accessed=size, transcendentals=0),
    )


def struct(shape, dtype):
    return jax.ShapeDtypeStruct(shape, dtype)


def pick_kernel(
    rhs, red, skel, interp, couple, inv, xr_out, ys_out, couple_out, inv_out,
    rhs_in, red_in, skel_in, interp_in, sems,
):
    groups, columns, total = rhs.shape
    block = interp.shape[1]
    ahead = [
        pltpu.make_async_copy(source, held, sems.at[groups + i])
        for i, (source, held) in enumerate(
            ((red, red_in), (skel, skel_in), (interp, interp_in), (inv, inv_out))
        )
    ]
    ahead += [
        pltpu.make_async_copy(couple.at[g], couple_out.at[g], sems.at[groups + 4 + g])
        for g in range(groups)
    ]
    boxes = [pltpu.make_async_copy(rhs.at[g], rhs_in.at[g], sems.at[g]) for g in range(groups)]
    for copy in ahead[:2] + boxes + ahead[2:]:
        copy.start()
    for copy in ahead[:2] + boxes + ahead[2:3]:
        copy.wait()
    own = own_part(skel_in[...], block)
    for g in range(groups):
        whole = rhs_in[g]
        high = whole.astype(BF16)
        low = (whole - high.astype(F32)).astype(BF16)
        xr = dot(high, onehot(red_in[g : g + 1, :], total)).astype(BF16)
        xr_out[g] = xr
        spots = onehot(own[g : g + 1, :], total)
        both = dot(jnp.concatenate([high, low], axis=0), spots)
        ys = both[:columns] + both[columns:] - dot_t(xr, interp_in[g])
        ys_out[:, g * block : (g + 1) * block] = ys
    for copy in ahead[3:]:
        copy.wait()


def leaf_kernel(rows, near, xr, ys, *refs):
    inv = refs[:rows]
    couple, red_out, own_out = refs[rows : rows + 3]
    sends = refs[rows + 3 : rows + 3 + 2 * REACH]
    acc = refs[-1]
    groups, slots = near.shape
    block = couple.shape[2]
    row = lax.axis_index("row")
    anchor = lax.axis_index("box")
    sign = 1 - 2 * (row % 2)
    acc[...] = jnp.zeros_like(acc)
    leaves = []
    for g in range(groups):
        parts = [dot_t(xr[g], inv[t][g]) for t in range(rows)]
        red_out[g] = parts[0]
        placed = []
        for place in range(rows):
            chosen = parts[0]
            for t in range(1, rows):
                chosen = jnp.where(row == (place ^ t), parts[t], chosen)
            placed.append(chosen)
        leaves.append(jnp.concatenate(placed, axis=1).astype(BF16))
    for g in range(groups):
        updates = dot_t(leaves[g], couple[g].reshape(slots * block, couple.shape[3]))
        for j in range(slots):
            target = near[g, j]
            clear = jnp.maximum(target, 0)
            section = (clear // groups - anchor) * sign + REACH
            spot = jnp.where(target >= 0, section * groups + clear % groups, acc.shape[0] - 1)
            acc[spot] += updates[:, j * block : (j + 1) * block]

    def merged(section):
        return jnp.concatenate([acc[section * groups + g] for g in range(groups)], axis=1)

    own_out[...] = ys[...] + merged(REACH)
    for ref, section in zip(sends, SECTIONS):
        ref[...] = merged(section + REACH).astype(BF16)


SECTIONS = (1, -1, 2, -2)


def sum_kernel(*refs):
    total = refs[0][...]
    for ref in refs[1:-2]:
        total = total + ref[...].astype(F32)
    refs[-2][...] = total
    refs[-1][...] = total.astype(BF16)


def shifted_index(index, half, rows, block, groups, skeletons):
    child, place = index // skeletons, index % skeletons
    piece = (place // block) ^ half
    return piece * (groups * block) + child * block + place % block


def parent_kernel(rows, near, red, *refs):
    pieces = refs[:rows]
    panel, xr_out = refs[rows : rows + 2]
    sends = refs[rows + 2 :]
    width = pieces[0].shape[1]
    redundant = red.shape[1]
    step = 128
    parent = jnp.concatenate([ref[...] for ref in pieces], axis=1)
    for start in range(0, redundant, step):
        stop = min(start + step, redundant)
        spots = onehot(red[:, start:stop], rows * width)
        xr_out[:, start:stop] = dot(parent, spots).astype(BF16)
    xr = xr_out[...]
    down = lax.axis_index("row") % 2
    for send, slot in zip(sends, (1 - down, down)):
        update = dot_t(xr, panel[0, slot])
        send[...] = jnp.where(near[0, slot] >= 0, update, 0.0).astype(BF16)


def finish_kernel(rows, skel, xr, interp, inv, own, *refs):
    pieces = refs[: rows - 1]
    red_out, ys_out = refs[rows - 1 :]
    width = own.shape[1]
    red_out[0] = dot_t(xr[...], inv[0])
    high = own[...].astype(BF16)
    low = (own[...] - high.astype(F32)).astype(BF16)
    spots = onehot(skel[...], rows * width)
    picked = dot(jnp.concatenate([high] + [ref[...] for ref in pieces], axis=1), spots)
    picked = picked + dot(low, spots[:width])
    ys_out[0] = picked - dot_t(xr[...], interp[0])


def shards(
    rhs, skel1, red1, interp1, inv1, couple1, near1, skel2, red2, interp2, inv2, panel2, near2
):
    rows = lax.axis_size("row")
    row = lax.axis_index("row")
    groups, columns, total = rhs.shape
    redundant, block = interp1.shape[1:]
    skeletons = skel1.shape[1]
    width = groups * block
    s2_block, i2_block = interp2.shape[2], inv2.shape[2]
    red2_count = red2.shape[1]

    inverse = row_pieces(turned(inv1))[1:]
    hbm = pl.BlockSpec(memory_space=pltpu.HBM)
    inv1, interp1, couple1 = turned(inv1), turned(interp1), turned(couple1)
    xr1, ys1, couple1, own_inv1 = pl.pallas_call(
        pick_kernel,
        out_shape=(
            struct((groups, columns, redundant), BF16),
            struct((columns, width), F32),
            struct(couple1.shape, BF16),
            struct(inv1.shape, BF16),
        ),
        in_specs=[hbm] * 6,
        scratch_shapes=[
            pltpu.VMEM(rhs.shape, F32),
            pltpu.VMEM(red1.shape, jnp.int32),
            pltpu.VMEM(skel1.shape, jnp.int32),
            pltpu.VMEM(interp1.shape, BF16),
            pltpu.SemaphoreType.DMA((2 * groups + 4,)),
        ],
        compiler_params=pltpu.CompilerParams(vmem_limit_bytes=48 << 20),
    )(*(pltpu.with_memory_space_constraint(v, pltpu.HBM) for v in (rhs, red1, skel1, interp1, couple1, inv1)))

    vmem = pl.BlockSpec(memory_space=pltpu.VMEM)
    red_one, own, *sends = pl.pallas_call(
        functools.partial(leaf_kernel, rows),
        out_shape=(
            struct((groups, columns, inv1.shape[1]), F32),
            struct((columns, width), F32),
        )
        + tuple(struct((columns, width), BF16) for _ in SECTIONS),
        in_specs=[pl.BlockSpec(memory_space=pltpu.SMEM)] + [vmem] * (rows + 3),
        scratch_shapes=[pltpu.VMEM(((2 * REACH + 1) * groups + 1, columns, block), F32)],
        compiler_params=pltpu.CompilerParams(vmem_limit_bytes=48 << 20),
    )(near1, xr1, ys1, own_inv1, *inverse, couple1)

    arrived = [
        box_permute(block_, abs(section), section < 0)
        for block_, section in zip(sends, SECTIONS)
    ]
    own_sum, own_high = call(
        sum_kernel, (struct((columns, width), F32), struct((columns, width), BF16))
    )(own, *arrived)
    pieces = row_pieces(own_high)

    place2 = functools.partial(
        shifted_index, half=row, rows=rows, block=block, groups=groups, skeletons=skeletons
    )
    own_skel2 = lax.dynamic_slice_in_dim(skel2, row * s2_block, s2_block, 1)
    xr2, send_up, send_down = pl.pallas_call(
        functools.partial(parent_kernel, rows),
        out_shape=(struct((columns, red2_count), BF16),)
        + tuple(struct((columns, s2_block), BF16) for _ in range(2)),
        in_specs=[pl.BlockSpec(memory_space=pltpu.SMEM)] + [vmem] * (rows + 2),
        compiler_params=pltpu.CompilerParams(vmem_limit_bytes=48 << 20),
    )(near2, place2(red2), *pieces, turned(panel2))
    moved = [box_permute(send_up, 1, False), box_permute(send_down, 1, True)]
    red_two, ys2 = call(
        functools.partial(finish_kernel, rows),
        (struct((1, columns, i2_block), F32), struct((1, columns, s2_block), F32)),
    )(place2(own_skel2), xr2, turned(interp2), turned(inv2), own_sum, *pieces[1:])
    skel_two = ys2 + moved[0].astype(F32)[None] + moved[1].astype(F32)[None]
    return red_one, red_two, skel_two


def solution(mesh):
    return jax.shard_map(
        shards,
        mesh=mesh,
        in_specs=(
            P("box", None, None),
            P("box", None),
            P("box", None),
            P("box", None, "row"),
            P("box", None, "row"),
            P("box", None, None, "row"),
            P("box", None),
            P("box", None),
            P("box", None),
            P("box", None, "row"),
            P("box", None, "row"),
            P("box", None, None, "row"),
            P("box", None),
        ),
        out_specs=(P("box", None, "row"), P("box", None, "row"), P("box", None, "row")),
        check_vma=False,
    )
```

time: 71 us -> 28.9 us (0.41)
  the two profiles are of different devices: /device:TPU:24 before, /device:TPU:6 now
where the time goes in v1:
time: 28.9 us; the launch traced here: 28.8 us
  waiting for transfers between devices  12.3 us (43%)
  Pallas kernels  8.43 us (29%)
  starting transfers between devices  6.38 us (22%)
  other arithmetic  0.82 us (3%)
  between operations  0.75 us (3%)
    ppermute x6, waiting for transfers between devices, box_permute(): return lax.ppermute(block, ('box', 'row'), route)  11.2 us
    ppermute x6, starting transfers between devices, box_permute(): return lax.ppermute(block, ('box', 'row'), route)  6.13 us
    pallas_call x1, Pallas kernels, shards(): pl.pallas_call(pick_kernel, out_shape=(struct((groups, columns, redundant...  2.86 us
    pallas_call x1, Pallas kernels, shards(): pl.pallas_call(functools.partial(leaf_kernel, rows), out_shape=(struct((g...  2.72 us
    pallas_call x1, Pallas kernels, shards(): pl.pallas_call(functools.partial(parent_kernel, rows), out_shape=(struct(...  1.54 us
    pallas_call x1, Pallas kernels, shards(): call(functools.partial(finish_kernel, rows), (struct((1, columns, i2_bloc...  1.25 us
    ppermute x2, waiting for transfers between devices, row_pieces(): lax.ppermute(block, 'row', [(i, i ^ t) for i in range(rows)])  1.1 us
    add x1, other arithmetic, shards(): skel_two = ys2 + moved[0].astype(F32)[None] + moved[1].astype(F32)[None]  0.64 us
  transfers between devices with their start and end apart: 8, of which 6 were waited for; matrix products, arithmetic and copies ran while one was open for 1% of the time, Pallas kernels for 14%

profile of v1, /device:TPU:6, one launch (start us, length us, event | category | flops | bytes accessed | tf_op | source)
XLA Modules:
  0.0 28.8 jit_solution(2001103730877225018)
XLA Ops:
  0.6 0.0 copy-start.3
  0.6 0.1 collective-permute-start
  0.7 2.9 %shard_map.148 = (bf16[8,64,128]{2,1,0:T(8,128)(2,1)S(1)}, f32[64,768]{1,0:T(8,128)S(1)}, bf16[8,8,96,128]{3,2,1,0:T(8,128)(2,1)S(1)}, bf16[8,64,128]{2,1,0:T(8,128)(2,1)S(1)}) custom-call(f32[8,64,320]{2,1,0:T(8,128)} %rhs.1, s32[8,128]{1,0:T(8,128)} %red.1, s32[8,192]{1,0:T(8,128)} %skel.1, bf16[8,96,128]{2,1,0:T(8,128)(2,1)} %bitcast.16, ...), custom_call_target="tpu_custom_call" | custom-call | tf_op jit(solution)/shard_map/pallas_call | solution.py:214
  3.6 0.0 copy-start.5
  3.6 0.0 copy-start.1
  3.6 0.0 copy-start.4
  3.6 0.0 collective-permute-done.refs_1_
  3.6 0.0 copy-done.3
  3.6 0.0 copy-start.6
  3.7 0.0 copy-start
  3.7 0.0 copy-start.2
  3.7 2.7 %shard_map.149 = (f32[8,64,64]{2,1,0:T(8,128)}, f32[64,768]{1,0:T(8,128)S(1)}, bf16[64,768]{1,0:T(8,128)(2,1)}, bf16[64,768]{1,0:T(8,128)(2,1)S(1)}, bf16[64,768...) custom-call(s32[8,8]{1,0:T(8,128)S(1)} %copy-done.3, bf16[8,64,128]{2,1,0:T(8,128)(2,1)S(1)} %get-tuple-element.20.xr, ...), custom_call_target="tpu_custom_call" | custom-call | tf_op jit(solution)/shard_map/pallas_call | solution.py:234
  6.4 1.5 %collective-permute-start.1 = (bf16[64,768]{1,0:T(8,128)(2,1)}, bf16[64,768]{1,0:T(8,128)(2,1)S(1)}, u32[]{:S(2)}, u32[]{:S(2)}) collective-permute-start(bf16[64,768]{1,0:T(8,128)(2,1)} %get-tuple-element.26), channel_id=1, source_target_pairs={{0,2},{1,0},{2,4},{3,1},{4,6},{5,3},{6,8},{7,5},{8,10},{9,7},{10,1... | collective-permute-start | bytes 294920 | tf_op jit(solution)/shard_map/ppermute | solution.py:32
  7.9 0.5 %collective-permute-start.2 = (bf16[64,768]{1,0:T(8,128)(2,1)S(1)}, bf16[64,768]{1,0:T(8,128)(2,1)S(1)}, u32[]{:S(2)}, u32[]{:S(2)}) collective-permute-start(bf16[64,768]{1,0:T(8,128)(2,1)S(1)} %get-tuple-element.27), channel_id=1, source_target_pairs={{0,1},{1,3},{2,0},{3,5},{4,2},{5,7},{6,4},{7,9},{8,6},{9,11},{10,8... | collective-permute-start | bytes 294920 | tf_op jit(solution)/shard_map/ppermute | solution.py:32
  8.4 1.5 %collective-permute-start.3 = (bf16[64,768]{1,0:T(8,128)(2,1)S(1)}, bf16[64,768]{1,0:T(8,128)(2,1)S(1)}, u32[]{:S(2)}, u32[]{:S(2)}) collective-permute-start(bf16[64,768]{1,0:T(8,128)(2,1)S(1)} %get-tuple-element.28), channel_id=1, source_target_pairs={{0,4},{1,0},{2,6},{3,2},{4,8},{5,1},{6,10},{7,3},{8,12},{9,5},{10,... | collective-permute-start | bytes 294920 | tf_op jit(solution)/shard_map/ppermute | solution.py:32
  9.9 0.5 %collective-permute-start.4 = (bf16[64,768]{1,0:T(8,128)(2,1)S(1)}, bf16[64,768]{1,0:T(8,128)(2,1)S(1)}, u32[]{:S(2)}, u32[]{:S(2)}) collective-permute-start(bf16[64,768]{1,0:T(8,128)(2,1)S(1)} %get-tuple-element.29), channel_id=1, source_target_pairs={{0,1},{1,5},{2,3},{3,7},{4,0},{5,9},{6,2},{7,11},{8,4},{9,13},{10,... | collective-permute-start | bytes 294920 | tf_op jit(solution)/shard_map/ppermute | solution.py:32
  10.5 1.8 %collective-permute-done.1.refs_1_ = bf16[64,768]{1,0:T(8,128)(2,1)S(1)} collective-permute-done((bf16[64,768]{1,0:T(8,128)(2,1)}, bf16[64,768]{1,0:T(8,128)(2,1)S(1)}, u32[]{:S(2)}, u32[]{:S(2)}) %collective-permute-start.1) | collective-permute-done | bytes 98336 | tf_op jit(solution)/shard_map/ppermute | solution.py:32
  12.2 3.4 %collective-permute-done.2.refs_2_ = bf16[64,768]{1,0:T(8,128)(2,1)S(1)} collective-permute-done((bf16[64,768]{1,0:T(8,128)(2,1)S(1)}, bf16[64,768]{1,0:T(8,128)(2,1)S(1)}, u32[]{:S(2)}, u32[]{:S(2)}) %collective-permute-start.2) | collective-permute-done | bytes 98336 | tf_op jit(solution)/shard_map/ppermute | solution.py:32
  15.6 2.1 %collective-permute-done.3.refs_3_ = bf16[64,768]{1,0:T(8,128)(2,1)S(1)} collective-permute-done((bf16[64,768]{1,0:T(8,128)(2,1)S(1)}, bf16[64,768]{1,0:T(8,128)(2,1)S(1)}, u32[]{:S(2)}, u32[]{:S(2)}) %collective-permute-start.3) | collective-permute-done | bytes 98336 | tf_op jit(solution)/shard_map/ppermute | solution.py:32
  17.7 0.0 collective-permute-done.4.refs_4_
  17.7 0.1 shard_map.150
  17.8 0.2 collective-permute-start.5
  18.0 0.0 copy-done.5
  18.0 0.1 fusion.red
  18.0 1.1 %collective-permute-done.5.refs_1_.refs_0_ = bf16[64,768]{1,0:T(8,128)(2,1)S(1)} collective-permute-done((bf16[64,768]{1,0:T(8,128)(2,1)S(1)}, bf16[64,768]{1,0:T(8,128)(2,1)S(1)}, u32[]{:S(2)}, u32[]{:S(2)}) %collective-permute-start.5) | collective-permute-done | bytes 98336 | tf_op jit(solution)/shard_map/ppermute | solution.py:18
  19.1 0.0 copy-done.1
  19.1 0.0 copy-done.4
  19.2 1.5 %shard_map.151 = (bf16[64,1152]{1,0:T(8,128)(2,1)S(1)}, bf16[64,192]{1,0:T(8,128)(2,1)S(1)}, bf16[64,192]{1,0:T(8,128)(2,1)S(1)}) custom-call(s32[1,2]{1,0:T(1,128)S(1)} %copy-done.4, s32[1,1152]{1,0:T(1,128)S(1)} %fusion.red, bf16[64,768]{1,0:T(8,128)(2,1)S(1)} %get-tuple-element.30.refs_0_, bf16[64,768]{1,0:T(8,128)(2,1)S(1)} %collective-permute-done.5.refs_1_.refs_0_, ...), custom_call_target="tpu_custom_call" | custom-call | tf_op jit(solution)/shard_map/pallas_call | solution.py:259
  20.7 1.7 %collective-permute-start.6 = (bf16[64,192]{1,0:T(8,128)(2,1)S(1)}, bf16[64,192]{1,0:T(8,128)(2,1)S(1)}, u32[]{:S(2)}, u32[]{:S(2)}) collective-permute-start(bf16[64,192]{1,0:T(8,128)(2,1)S(1)} %get-tuple-element.35), channel_id=1, source_target_pairs={{0,2},{1,0},{2,4},{3,1},{4,6},{5,3},{6,8},{7,5},{8,10},{9,7},{10,1... | collective-permute-start | bytes 73736 | tf_op jit(solution)/shard_map/ppermute | solution.py:32
  22.4 0.4 %collective-permute-start.7 = (bf16[64,192]{1,0:T(8,128)(2,1)S(1)}, bf16[64,192]{1,0:T(8,128)(2,1)S(1)}, u32[]{:S(2)}, u32[]{:S(2)}) collective-permute-start(bf16[64,192]{1,0:T(8,128)(2,1)S(1)} %get-tuple-element.36), channel_id=1, source_target_pairs={{0,1},{1,3},{2,0},{3,5},{4,2},{5,7},{6,4},{7,9},{8,6},{9,11},{10,8... | collective-permute-start | bytes 73736 | tf_op jit(solution)/shard_map/ppermute | solution.py:32
  22.8 0.0 copy-done.6
  22.8 0.1 fusion.1.skel
  22.9 0.0 copy-done
  22.9 0.0 copy-done.2
  22.9 1.3 %shard_map.152 = (f32[1,64,576]{2,1,0:T(8,128)}, f32[1,64,192]{2,1,0:T(8,128)S(1)}) custom-call(s32[1,192]{1,0:T(1,128)S(1)} %fusion.1.skel, bf16[64,1152]{1,0:T(8,128)(2,1)S(1)} %get-tuple-element.31.xr, bf16[1,192,1152]{2,1,0:T(8,128)(2,1)S(1)} %bitcast.14, bf16[1,576,1152]{2,1,0:T(8,128)(2,1)S(1)} %bitcast.12, f32[64,768]{1,0:T(8,128)S(1)} %get-tuple-element.32.own, ...), custom_call_target="tpu_custom_call" | custom-call | tf_op jit(solution)/shard_map/pallas_call | solution.py:267
  24.2 0.5 %collective-permute-done.6 = bf16[64,192]{1,0:T(8,128)(2,1)S(1)} collective-permute-done((bf16[64,192]{1,0:T(8,128)(2,1)S(1)}, bf16[64,192]{1,0:T(8,128)(2,1)S(1)}, u32[]{:S(2)}, u32[]{:S(2)}) %collective-permute-start.6) | collective-permute-done | bytes 24608 | tf_op jit(solution)/shard_map/ppermute | solution.py:32
  24.7 3.4 %collective-permute-done.7 = bf16[64,192]{1,0:T(8,128)(2,1)S(1)} collective-permute-done((bf16[64,192]{1,0:T(8,128)(2,1)S(1)}, bf16[64,192]{1,0:T(8,128)(2,1)S(1)}, u32[]{:S(2)}, u32[]{:S(2)}) %collective-permute-start.7) | collective-permute-done | bytes 24608 | tf_op jit(solution)/shard_map/ppermute | solution.py:32
  28.1 0.6 %convert_add_fusion = f32[1,64,192]{2,1,0:T(8,128)} fusion(f32[1,64,192]{2,1,0:T(8,128)S(1)} %get-tuple-element.34, bf16[64,192]{1,0:T(8,128)(2,1)S(1)} %collective-permute-done.7, bf16[64,192]{1,0:T(8,128)(2,1)S(1)} %collective-permute-done.6), kind=kLoop, calls=%fused_computation | loop fusion | flops 49152 | bytes 147456 | tf_op jit(solution)/shard_map/add | solution.py:271
Async XLA Ops:
  0.6 3.0 %copy-start.3 = (s32[8,8]{1,0:T(8,128)S(1)}, s32[8,8]{1,0:T(8,128)}, u32[]{:S(2)}) copy-start(s32[8,8]{1,0:T(8,128)} %near.2) | copy-start | bytes 772
  0.6 3.0 %collective-permute-start = (bf16[8,64,128]{2,1,0:T(8,128)(2,1)}, bf16[8,64,128]{2,1,0:T(8,128)(2,1)S(1)}, u32[]{:S(2)}, u32[]{:S(2)}) collective-permute-start(bf16[8,64,128]{2,1,0:T(8,128)(2,1)} %bitcast.17), channel_id=1, source_target_pairs={{0,1},{1,0},{2,3},{3,2},{4,5},{5,4},{6,7},{7,6},{8,9},{9,8},{10,11... | collective-permute-start | bytes 393224 | tf_op jit(solution)/shard_map/ppermute | solution.py:18
  3.6 14.4 %copy-start.5 = (s32[1,1152]{1,0:T(1,128)S(1)}, s32[1,1152]{1,0:T(1,128)}, u32[]{:S(2)}) copy-start(s32[1,1152]{1,0:T(1,128)} %param.21) | copy-start | bytes 13828
  3.6 15.5 %copy-start.1 = (bf16[1,2,1152,192]{2,3,1,0:T(8,128)(2,1)S(1)}, bf16[1,2,1152,192]{2,3,1,0:T(8,128)(2,1)}, u32[]{:S(2)}) copy-start(bf16[1,2,1152,192]{2,3,1,0:T(8,128)(2,1)} %param.24) | copy-start | bytes 2654212
  3.6 15.5 %copy-start.4 = (s32[1,2]{1,0:T(1,128)S(1)}, s32[1,2]{1,0:T(1,128)}, u32[]{:S(2)}) copy-start(s32[1,2]{1,0:T(1,128)} %near.3) | copy-start | bytes 28
  3.6 19.1 %copy-start.6 = (s32[1,384]{1,0:T(1,128)S(1)}, s32[1,384]{1,0:T(1,128)}, u32[]{:S(2)}) copy-start(s32[1,384]{1,0:T(1,128)} %param.20) | copy-start | bytes 4612
  3.7 19.2 %copy-start = (bf16[1,1152,576]{1,2,0:T(8,128)(2,1)S(1)}, bf16[1,1152,576]{1,2,0:T(8,128)(2,1)}, u32[]{:S(2)}) copy-start(bf16[1,1152,576]{1,2,0:T(8,128)(2,1)} %param.23) | copy-start | bytes 3981316
  3.7 19.2 %copy-start.2 = (bf16[1,1152,192]{1,2,0:T(8,128)(2,1)S(1)}, bf16[1,1152,192]{1,2,0:T(8,128)(2,1)}, u32[]{:S(2)}) copy-start(bf16[1,1152,192]{1,2,0:T(8,128)(2,1)} %param.22) | copy-start | bytes 1327108
  6.4 5.8 %collective-permute-start.1 = (bf16[64,768]{1,0:T(8,128)(2,1)}, bf16[64,768]{1,0:T(8,128)(2,1)S(1)}, u32[]{:S(2)}, u32[]{:S(2)}) collective-permute-start(bf16[64,768]{1,0:T(8,128)(2,1)} %get-tuple-element.26), channel_id=1, source_target_pairs={{0,2},{1,0},{2,4},{3,1},{4,6},{5,3},{6,8},{7,5},{8,10},{9,7},{10,1... | collective-permute-start | bytes 294920 | tf_op jit(solution)/shard_map/ppermute | solution.py:32
  7.9 7.7 %collective-permute-start.2 = (bf16[64,768]{1,0:T(8,128)(2,1)S(1)}, bf16[64,768]{1,0:T(8,128)(2,1)S(1)}, u32[]{:S(2)}, u32[]{:S(2)}) collective-permute-start(bf16[64,768]{1,0:T(8,128)(2,1)S(1)} %get-tuple-element.27), channel_id=1, source_target_pairs={{0,1},{1,3},{2,0},{3,5},{4,2},{5,7},{6,4},{7,9},{8,6},{9,11},{10,8... | collective-permute-start | bytes 294920 | tf_op jit(solution)/shard_map/ppermute | solution.py:32
  8.4 9.3 %collective-permute-start.3 = (bf16[64,768]{1,0:T(8,128)(2,1)S(1)}, bf16[64,768]{1,0:T(8,128)(2,1)S(1)}, u32[]{:S(2)}, u32[]{:S(2)}) collective-permute-start(bf16[64,768]{1,0:T(8,128)(2,1)S(1)} %get-tuple-element.28), channel_id=1, source_target_pairs={{0,4},{1,0},{2,6},{3,2},{4,8},{5,1},{6,10},{7,3},{8,12},{9,5},{10,... | collective-permute-start | bytes 294920 | tf_op jit(solution)/shard_map/ppermute | solution.py:32
  9.9 7.8 %collective-permute-start.4 = (bf16[64,768]{1,0:T(8,128)(2,1)S(1)}, bf16[64,768]{1,0:T(8,128)(2,1)S(1)}, u32[]{:S(2)}, u32[]{:S(2)}) collective-permute-start(bf16[64,768]{1,0:T(8,128)(2,1)S(1)} %get-tuple-element.29), channel_id=1, source_target_pairs={{0,1},{1,5},{2,3},{3,7},{4,0},{5,9},{6,2},{7,11},{8,4},{9,13},{10,... | collective-permute-start | bytes 294920 | tf_op jit(solution)/shard_map/ppermute | solution.py:32
  17.8 1.4 %collective-permute-start.5 = (bf16[64,768]{1,0:T(8,128)(2,1)S(1)}, bf16[64,768]{1,0:T(8,128)(2,1)S(1)}, u32[]{:S(2)}, u32[]{:S(2)}) collective-permute-start(bf16[64,768]{1,0:T(8,128)(2,1)S(1)} %get-tuple-element.30.refs_0_), channel_id=1, source_target_pairs={{0,1},{1,0},{2,3},{3,2},{4,5},{5,4},{6,7},{7,6},{8,9},{9,8},{10,11... | collective-permute-start | bytes 294920 | tf_op jit(solution)/shard_map/ppermute | solution.py:18
  20.7 4.0 %collective-permute-start.6 = (bf16[64,192]{1,0:T(8,128)(2,1)S(1)}, bf16[64,192]{1,0:T(8,128)(2,1)S(1)}, u32[]{:S(2)}, u32[]{:S(2)}) collective-permute-start(bf16[64,192]{1,0:T(8,128)(2,1)S(1)} %get-tuple-element.35), channel_id=1, source_target_pairs={{0,2},{1,0},{2,4},{3,1},{4,6},{5,3},{6,8},{7,5},{8,10},{9,7},{10,1... | collective-permute-start | bytes 73736 | tf_op jit(solution)/shard_map/ppermute | solution.py:32
  22.4 5.7 %collective-permute-start.7 = (bf16[64,192]{1,0:T(8,128)(2,1)S(1)}, bf16[64,192]{1,0:T(8,128)(2,1)S(1)}, u32[]{:S(2)}, u32[]{:S(2)}) collective-permute-start(bf16[64,192]{1,0:T(8,128)(2,1)S(1)} %get-tuple-element.36), channel_id=1, source_target_pairs={{0,1},{1,3},{2,0},{3,5},{4,2},{5,7},{6,4},{7,9},{8,6},{9,11},{10,8... | collective-permute-start | bytes 73736 | tf_op jit(solution)/shard_map/ppermute | solution.py:32

commit v2 on v1

--- a/solution.py
+++ b/solution.py
@@ -56,16 +56,6 @@
         part = values[:, place * block : (place + 1) * block]
         chosen = jnp.where(row == place, part, chosen)
     return chosen
-
-
-def call(body, out_shape, scratch=(), vmem=48 << 20, flops=0, size=0):
-    return pl.pallas_call(
-        body,
-        out_shape=out_shape,
-        scratch_shapes=list(scratch),
-        compiler_params=pltpu.CompilerParams(vmem_limit_bytes=vmem),
-        cost_estimate=pl.CostEstimate(flops=flops, bytes_accessed=size, transcendentals=0),
-    )
 
 
 def struct(shape, dtype):
@@ -108,11 +98,13 @@
         copy.wait()
 
 
-def leaf_kernel(rows, near, xr, ys, *refs):
+def leaf_kernel(rows, near_held, xr, ys, *refs):
     inv = refs[:rows]
-    couple, red_out, own_out = refs[rows : rows + 3]
-    sends = refs[rows + 3 : rows + 3 + 2 * REACH]
-    acc = refs[-1]
+    couple, own_out = refs[rows : rows + 2]
+    sends = refs[rows + 2 : rows + 2 + 2 * REACH]
+    acc, near, sem = refs[-3:]
+    fetch = pltpu.make_async_copy(near_held, near, sem)
+    fetch.start()
     groups, slots = near.shape
     block = couple.shape[2]
     row = lax.axis_index("row")
@@ -122,7 +114,6 @@
     leaves = []
     for g in range(groups):
         parts = [dot_t(xr[g], inv[t][g]) for t in range(rows)]
-        red_out[g] = parts[0]
         placed = []
         for place in range(rows):
             chosen = parts[0]
@@ -130,6 +121,7 @@
                 chosen = jnp.where(row == (place ^ t), parts[t], chosen)
             placed.append(chosen)
         leaves.append(jnp.concatenate(placed, axis=1).astype(BF16))
+    fetch.wait()
     for g in range(groups):
         updates = dot_t(leaves[g], couple[g].reshape(slots * block, couple.shape[3]))
         for j in range(slots):
@@ -150,50 +142,43 @@
 SECTIONS = (1, -1, 2, -2)
 
 
-def sum_kernel(*refs):
-    total = refs[0][...]
-    for ref in refs[1:-2]:
-        total = total + ref[...].astype(F32)
-    refs[-2][...] = total
-    refs[-1][...] = total.astype(BF16)
-
-
-def shifted_index(index, half, rows, block, groups, skeletons):
+def shifted_index(index, half, block, groups, skeletons):
     child, place = index // skeletons, index % skeletons
     piece = (place // block) ^ half
     return piece * (groups * block) + child * block + place % block
 
 
-def parent_kernel(rows, near, red, *refs):
-    pieces = refs[:rows]
-    panel, xr_out = refs[rows : rows + 2]
-    sends = refs[rows + 2 :]
-    width = pieces[0].shape[1]
-    redundant = red.shape[1]
-    step = 128
-    parent = jnp.concatenate([ref[...] for ref in pieces], axis=1)
-    for start in range(0, redundant, step):
-        stop = min(start + step, redundant)
-        spots = onehot(red[:, start:stop], rows * width)
-        xr_out[:, start:stop] = dot(parent, spots).astype(BF16)
-    xr = xr_out[...]
+def spread_kernel(near, red, panel, xr, inv1, red_out, out):
+    for g in range(xr.shape[0]):
+        red_out[g] = dot_t(xr[g], inv1[g])
+    spots = onehot(red[...], out.shape[1])
+    for slot in range(out.shape[0]):
+        spread = dot_t(spots, panel[0, slot])
+        out[slot] = jnp.where(near[0, slot] >= 0, spread, 0.0).astype(BF16)
+
+
+def sum_kernel(own, *refs):
+    total = own[...]
+    for ref in refs[:-1]:
+        total = total + ref[...].astype(F32)
+    refs[-1][...] = total.astype(BF16)
+
+
+def update_kernel(panel, *refs):
+    pieces, sends = refs[:-2], refs[-2:]
+    parent = jnp.concatenate([piece[...] for piece in pieces], axis=1)
     down = lax.axis_index("row") % 2
     for send, slot in zip(sends, (1 - down, down)):
-        update = dot_t(xr, panel[0, slot])
-        send[...] = jnp.where(near[0, slot] >= 0, update, 0.0).astype(BF16)
-
-
-def finish_kernel(rows, skel, xr, interp, inv, own, *refs):
-    pieces = refs[: rows - 1]
-    red_out, ys_out = refs[rows - 1 :]
-    width = own.shape[1]
-    red_out[0] = dot_t(xr[...], inv[0])
-    high = own[...].astype(BF16)
-    low = (own[...] - high.astype(F32)).astype(BF16)
-    spots = onehot(skel[...], rows * width)
-    picked = dot(jnp.concatenate([high] + [ref[...] for ref in pieces], axis=1), spots)
-    picked = picked + dot(low, spots[:width])
-    ys_out[0] = picked - dot_t(xr[...], interp[0])
+        send[...] = dot(parent, panel[slot]).astype(BF16)
+
+
+def finish_kernel(red, skel, inv, interp, *refs):
+    pieces, (red_out, ys_out) = refs[:-2], refs[-2:]
+    parent = jnp.concatenate([piece[...] for piece in pieces], axis=1)
+    count = parent.shape[1]
+    xr = dot(parent, onehot(red[...], count)).astype(BF16)
+    red_out[0] = dot_t(xr, inv[0])
+    ys_out[0] = dot(parent, onehot(skel[...], count)) - dot_t(xr, interp[0])
 
 
 def shards(
@@ -231,43 +216,54 @@
     )(*(pltpu.with_memory_space_constraint(v, pltpu.HBM) for v in (rhs, red1, skel1, interp1, couple1, inv1)))
 
     vmem = pl.BlockSpec(memory_space=pltpu.VMEM)
-    red_one, own, *sends = pl.pallas_call(
+    smem = pl.BlockSpec(memory_space=pltpu.SMEM)
+    params = pltpu.CompilerParams(vmem_limit_bytes=48 << 20)
+    send = struct((columns, width), BF16)
+    own, *sends = pl.pallas_call(
         functools.partial(leaf_kernel, rows),
+        out_shape=(struct((columns, width), F32),) + (send,) * len(SECTIONS),
+        in_specs=[vmem] * (rows + 4),
+        scratch_shapes=[
+            pltpu.VMEM(((2 * REACH + 1) * groups + 1, columns, block), F32),
+            pltpu.SMEM(near1.shape, jnp.int32),
+            pltpu.SemaphoreType.DMA,
+        ],
+        compiler_params=params,
+    )(near1, xr1, ys1, own_inv1, *inverse, couple1)
+
+    arrived = [
+        box_permute(piece, abs(section), section < 0) for piece, section in zip(sends, SECTIONS)
+    ]
+
+    place2 = functools.partial(
+        shifted_index, half=row, block=block, groups=groups, skeletons=skeletons
+    )
+    red_place, skel_place = place2(red2), place2(
+        lax.dynamic_slice_in_dim(skel2, row * s2_block, s2_block, 1)
+    )
+    red_one, panel_spread = pl.pallas_call(
+        spread_kernel,
         out_shape=(
             struct((groups, columns, inv1.shape[1]), F32),
-            struct((columns, width), F32),
-        )
-        + tuple(struct((columns, width), BF16) for _ in SECTIONS),
-        in_specs=[pl.BlockSpec(memory_space=pltpu.SMEM)] + [vmem] * (rows + 3),
-        scratch_shapes=[pltpu.VMEM(((2 * REACH + 1) * groups + 1, columns, block), F32)],
-        compiler_params=pltpu.CompilerParams(vmem_limit_bytes=48 << 20),
-    )(near1, xr1, ys1, own_inv1, *inverse, couple1)
-
-    arrived = [
-        box_permute(block_, abs(section), section < 0)
-        for block_, section in zip(sends, SECTIONS)
-    ]
-    own_sum, own_high = call(
-        sum_kernel, (struct((columns, width), F32), struct((columns, width), BF16))
-    )(own, *arrived)
-    pieces = row_pieces(own_high)
-
-    place2 = functools.partial(
-        shifted_index, half=row, rows=rows, block=block, groups=groups, skeletons=skeletons
-    )
-    own_skel2 = lax.dynamic_slice_in_dim(skel2, row * s2_block, s2_block, 1)
-    xr2, send_up, send_down = pl.pallas_call(
-        functools.partial(parent_kernel, rows),
-        out_shape=(struct((columns, red2_count), BF16),)
-        + tuple(struct((columns, s2_block), BF16) for _ in range(2)),
-        in_specs=[pl.BlockSpec(memory_space=pltpu.SMEM)] + [vmem] * (rows + 2),
-        compiler_params=pltpu.CompilerParams(vmem_limit_bytes=48 << 20),
-    )(near2, place2(red2), *pieces, turned(panel2))
-    moved = [box_permute(send_up, 1, False), box_permute(send_down, 1, True)]
-    red_two, ys2 = call(
-        functools.partial(finish_kernel, rows),
-        (struct((1, columns, i2_block), F32), struct((1, columns, s2_block), F32)),
-    )(place2(own_skel2), xr2, turned(interp2), turned(inv2), own_sum, *pieces[1:])
+            struct((near2.shape[1], rows * width, s2_block), BF16),
+        ),
+        in_specs=[smem] + [vmem] * 4,
+        compiler_params=params,
+    )(near2, red_place, turned(panel2), xr1, own_inv1)
+    own, panel_spread = lax.optimization_barrier((own, panel_spread))
+    high = pl.pallas_call(sum_kernel, out_shape=send, compiler_params=params)(own, *arrived)
+    pieces = row_pieces(high)
+    updates = pl.pallas_call(
+        update_kernel,
+        out_shape=(struct((columns, s2_block), BF16),) * 2,
+        compiler_params=params,
+    )(panel_spread, *pieces)
+    moved = [box_permute(piece, 1, flip) for piece, flip in zip(updates, (False, True))]
+    red_two, ys2 = pl.pallas_call(
+        finish_kernel,
+        out_shape=(struct((1, columns, i2_block), F32), struct((1, columns, s2_block), F32)),
+        compiler_params=params,
+    )(red_place, skel_place, turned(inv2), turned(interp2), *pieces)
     skel_two = ys2 + moved[0].astype(F32)[None] + moved[1].astype(F32)[None]
     return red_one, red_two, skel_two
 

time: 28.9 us -> 26.9 us (0.931)
  waiting for transfers between devices: 12.3 us -> 8.43 us
  Pallas kernels: 8.43 us -> 10.2 us
    ppermute x6, waiting for transfers between devices: 11.2 us -> 7.26 us  [box_permute(): return lax.ppermute(block, ('box', 'row'), route)]
    pallas_call x4 -> x5, Pallas kernels: 5.57 us -> 7.35 us  [the longest x1 3.14 us: shards(): pl.pallas_call(spread_kernel, out_shape=(struct((groups, columns, inv1.sh...]
  transfers between devices with their start and end apart: 8 -> 8, of which waited for: 6 -> 4; matrix products, arithmetic and copies ran while one was open for 1% -> 1% of each run, Pallas kernels for 14% -> 30%
where the time goes in v2:
time: 26.9 us; the launch traced here: 26.8 us
  Pallas kernels  10.2 us (38%)
  waiting for transfers between devices  8.43 us (31%)
  starting transfers between devices  6.46 us (24%)
  other arithmetic  0.82 us (3%)
  between operations  0.79 us (3%)
    ppermute x6, waiting for transfers between devices, box_permute(): return lax.ppermute(block, ('box', 'row'), route)  7.26 us
    ppermute x6, starting transfers between devices, box_permute(): return lax.ppermute(block, ('box', 'row'), route)  6.19 us
    pallas_call x1, Pallas kernels, shards(): pl.pallas_call(spread_kernel, out_shape=(struct((groups, columns, inv1.sh...  3.14 us
    pallas_call x1, Pallas kernels, shards(): pl.pallas_call(pick_kernel, out_shape=(struct((groups, columns, redundant...  2.87 us
    pallas_call x1, Pallas kernels, shards(): pl.pallas_call(finish_kernel, out_shape=(struct((1, columns, i2_block), F...  1.91 us
    pallas_call x1, Pallas kernels, shards(): pl.pallas_call(functools.partial(leaf_kernel, rows), out_shape=(struct((c...  1.84 us
    ppermute x2, waiting for transfers between devices, row_pieces(): lax.ppermute(block, 'row', [(i, i ^ t) for i in range(rows)])  1.17 us
    add x1, other arithmetic, shards(): skel_two = ys2 + moved[0].astype(F32)[None] + moved[1].astype(F32)[None]  0.64 us
  transfers between devices with their start and end apart: 8, of which 4 were waited for; matrix products, arithmetic and copies ran while one was open for 1% of the time, Pallas kernels for 30%

profile of v2, /device:TPU:6, one launch (start us, length us, event | category | flops | bytes accessed | tf_op | source)
XLA Modules:
  0.0 26.8 jit_solution(7721171377655869882)
XLA Ops:
  0.6 0.0 copy-start.3
  0.6 0.1 collective-permute-start
  0.7 2.9 %shard_map.148 = (bf16[8,64,128]{2,1,0:T(8,128)(2,1)S(1)}, f32[64,768]{1,0:T(8,128)S(1)}, bf16[8,8,96,128]{3,2,1,0:T(8,128)(2,1)S(1)}, bf16[8,64,128]{2,1,0:T(8,128)(2,1)S(1)}) custom-call(f32[8,64,320]{2,1,0:T(8,128)} %rhs.1, s32[8,128]{1,0:T(8,128)} %red.1, s32[8,192]{1,0:T(8,128)} %skel.1, bf16[8,96,128]{2,1,0:T(8,128)(2,1)} %bitcast.16, ...), custom_call_target="tpu_custom_call" | custom-call | tf_op jit(solution)/shard_map/pallas_call | solution.py:199
  3.6 0.0 copy-start.5
  3.6 0.0 copy-start.1
  3.6 0.0 copy-start.4
  3.6 0.0 collective-permute-done.refs_1_
  3.6 0.0 copy-done.3
  3.7 1.8 %shard_map.150 = (f32[64,768]{1,0:T(8,128)S(1)}, bf16[64,768]{1,0:T(8,128)(2,1)S(1)}, bf16[64,768]{1,0:T(8,128)(2,1)S(1)}, bf16[64,768]{1,0:T(8,128)(2,1)S(1)}, bf16[64,768]{1,0:T(8,128)(2,1)S(1)}) custom-call(s32[8,8]{1,0:T(8,128)S(1)} %copy-done.3, bf16[8,64,128]{2,1,0:T(8,128)(2,1)S(1)} %get-tuple-element.20.xr, f32[64,768]{1,0:T(8,128)S(1)} %get-tuple-element.23.ys, ...), custom_call_target="tpu_custom_call" | custom-call | tf_op jit(solution)/shard_map/pallas_call | solution.py:222
  5.5 1.5 %collective-permute-start.1 = (bf16[64,768]{1,0:T(8,128)(2,1)S(1)}, bf16[64,768]{1,0:T(8,128)(2,1)S(1)}, u32[]{:S(2)}, u32[]{:S(2)}) collective-permute-start(bf16[64,768]{1,0:T(8,128)(2,1)S(1)} %get-tuple-element.28), channel_id=1, source_target_pairs={{0,2},{1,0},{2,4},{3,1},{4,6},{5,3},{6,8},{7,5},{8,10},{9,7},{10,1... | collective-permute-start | bytes 294920 | tf_op jit(solution)/shard_map/ppermute | solution.py:32
  7.0 0.5 %collective-permute-start.2 = (bf16[64,768]{1,0:T(8,128)(2,1)S(1)}, bf16[64,768]{1,0:T(8,128)(2,1)S(1)}, u32[]{:S(2)}, u32[]{:S(2)}) collective-permute-start(bf16[64,768]{1,0:T(8,128)(2,1)S(1)} %get-tuple-element.29), channel_id=1, source_target_pairs={{0,1},{1,3},{2,0},{3,5},{4,2},{5,7},{6,4},{7,9},{8,6},{9,11},{10,8... | collective-permute-start | bytes 294920 | tf_op jit(solution)/shard_map/ppermute | solution.py:32
  7.6 1.5 %collective-permute-start.3 = (bf16[64,768]{1,0:T(8,128)(2,1)S(1)}, bf16[64,768]{1,0:T(8,128)(2,1)S(1)}, u32[]{:S(2)}, u32[]{:S(2)}) collective-permute-start(bf16[64,768]{1,0:T(8,128)(2,1)S(1)} %get-tuple-element.30), channel_id=1, source_target_pairs={{0,4},{1,0},{2,6},{3,2},{4,8},{5,1},{6,10},{7,3},{8,12},{9,5},{10,... | collective-permute-start | bytes 294920 | tf_op jit(solution)/shard_map/ppermute | solution.py:32
  9.1 0.5 %collective-permute-start.4 = (bf16[64,768]{1,0:T(8,128)(2,1)S(1)}, bf16[64,768]{1,0:T(8,128)(2,1)S(1)}, u32[]{:S(2)}, u32[]{:S(2)}) collective-permute-start(bf16[64,768]{1,0:T(8,128)(2,1)S(1)} %get-tuple-element.31), channel_id=1, source_target_pairs={{0,1},{1,5},{2,3},{3,7},{4,0},{5,9},{6,2},{7,11},{8,4},{9,13},{10,... | collective-permute-start | bytes 294920 | tf_op jit(solution)/shard_map/ppermute | solution.py:32
  9.6 0.0 copy-done.5
  9.6 0.1 fusion.red
  9.7 0.0 copy-done.1
  9.7 0.0 copy-done.4
  9.7 0.0 copy-start.6
  9.7 0.0 copy-start
  9.7 0.0 copy-start.2
  9.8 3.1 %shard_map.149 = (f32[8,64,64]{2,1,0:T(8,128)}, bf16[2,1536,192]{2,1,0:T(8,128)(2,1)S(1)}) custom-call(s32[1,2]{1,0:T(1,128)S(1)} %copy-done.4, s32[1,1152]{1,0:T(1,128)S(1)} %fusion.red, bf16[1,2,192,1152]{3,2,1,0:T(8,128)(2,1)S(1)} %bitcast.13, bf16[8,64,128]{2,1,0:T(8,128)(2,1)S(1)} %get-tuple-element.20.xr, ...), custom_call_target="tpu_custom_call" | custom-call | tf_op jit(solution)/shard_map/pallas_call | solution.py:244
  12.9 0.0 collective-permute-done.1.refs_0_
  12.9 1.7 %collective-permute-done.2.refs_1_ = bf16[64,768]{1,0:T(8,128)(2,1)S(1)} collective-permute-done((bf16[64,768]{1,0:T(8,128)(2,1)S(1)}, bf16[64,768]{1,0:T(8,128)(2,1)S(1)}, u32[]{:S(2)}, u32[]{:S(2)}) %collective-permute-start.2) | collective-permute-done | bytes 98336 | tf_op jit(solution)/shard_map/ppermute | solution.py:32
  14.6 2.0 %collective-permute-done.3.refs_2_ = bf16[64,768]{1,0:T(8,128)(2,1)S(1)} collective-permute-done((bf16[64,768]{1,0:T(8,128)(2,1)S(1)}, bf16[64,768]{1,0:T(8,128)(2,1)S(1)}, u32[]{:S(2)}, u32[]{:S(2)}) %collective-permute-start.3) | collective-permute-done | bytes 98336 | tf_op jit(solution)/shard_map/ppermute | solution.py:32
  16.6 0.0 collective-permute-done.4.refs_3_
  16.6 0.1 shard_map.151.refs_0_
  16.6 0.2 collective-permute-start.5
  16.8 1.2 %collective-permute-done.5.refs_1_ = bf16[64,768]{1,0:T(8,128)(2,1)S(1)} collective-permute-done((bf16[64,768]{1,0:T(8,128)(2,1)S(1)}, bf16[64,768]{1,0:T(8,128)(2,1)S(1)}, u32[]{:S(2)}, u32[]{:S(2)}) %collective-permute-start.5) | collective-permute-done | bytes 98336 | tf_op jit(solution)/shard_map/ppermute | solution.py:18
  18.0 0.4 %shard_map.153 = (bf16[64,192]{1,0:T(8,128)(2,1)S(1)}, bf16[64,192]{1,0:T(8,128)(2,1)S(1)}) custom-call(bf16[2,1536,192]{2,1,0:T(8,128)(2,1)S(1)} %get-tuple-element.34.panel, bf16[64,768]{1,0:T(8,128)(2,1)S(1)} %shard_map.151.refs_0_, bf16[64,768]{1,0:T(8,128)(2,1)S(1)} %collective-permute-done.5.refs_1_), custom_call_target="tpu_custom_call" | custom-call | tf_op jit(solution)/shard_map/pallas_call | solution.py:256
  18.4 2.0 %collective-permute-start.6 = (bf16[64,192]{1,0:T(8,128)(2,1)S(1)}, bf16[64,192]{1,0:T(8,128)(2,1)S(1)}, u32[]{:S(2)}, u32[]{:S(2)}) collective-permute-start(bf16[64,192]{1,0:T(8,128)(2,1)S(1)} %get-tuple-element.35), channel_id=1, source_target_pairs={{0,2},{1,0},{2,4},{3,1},{4,6},{5,3},{6,8},{7,5},{8,10},{9,7},{10,1... | collective-permute-start | bytes 73736 | tf_op jit(solution)/shard_map/ppermute | solution.py:32
  20.4 0.1 collective-permute-start.7
  20.5 0.0 copy-done.6
  20.5 0.1 fusion.1.skel
  20.6 0.0 copy-done
  20.6 0.0 copy-done.2
  20.6 1.9 %shard_map.152 = (f32[1,64,576]{2,1,0:T(8,128)}, f32[1,64,192]{2,1,0:T(8,128)S(1)}) custom-call(s32[1,1152]{1,0:T(1,128)S(1)} %fusion.red, s32[1,192]{1,0:T(1,128)S(1)} %fusion.1.skel, bf16[1,576,1152]{2,1,0:T(8,128)(2,1)S(1)} %bitcast.12, bf16[1,192,1152]{2,1,0:T(8,128)(2,1)S(1)} %bitcast.14, bf16[64,768]{1,0:T(8,128)(2,1)S(1)} %shard_map.151.refs_0_, ...), custom_call_target="tpu_custom_call" | custom-call | tf_op jit(solution)/shard_map/pallas_call | solution.py:262
  22.5 0.0 collective-permute-done.6
  22.5 3.6 %collective-permute-done.7 = bf16[64,192]{1,0:T(8,128)(2,1)S(1)} collective-permute-done((bf16[64,192]{1,0:T(8,128)(2,1)S(1)}, bf16[64,192]{1,0:T(8,128)(2,1)S(1)}, u32[]{:S(2)}, u32[]{:S(2)}) %collective-permute-start.7) | collective-permute-done | bytes 24608 | tf_op jit(solution)/shard_map/ppermute | solution.py:32
  26.1 0.6 %convert_add_fusion = f32[1,64,192]{2,1,0:T(8,128)} fusion(f32[1,64,192]{2,1,0:T(8,128)S(1)} %get-tuple-element.33, bf16[64,192]{1,0:T(8,128)(2,1)S(1)} %collective-permute-done.7, bf16[64,192]{1,0:T(8,128)(2,1)S(1)} %collective-permute-done.6), kind=kLoop, calls=%fused_computation | loop fusion | flops 49152 | bytes 147456 | tf_op jit(solution)/shard_map/add | solution.py:267
Async XLA Ops:
  0.6 3.0 %copy-start.3 = (s32[8,8]{1,0:T(8,128)S(1)}, s32[8,8]{1,0:T(8,128)}, u32[]{:S(2)}) copy-start(s32[8,8]{1,0:T(8,128)} %near_held.1) | copy-start | bytes 772
  0.6 3.0 %collective-permute-start = (bf16[8,64,128]{2,1,0:T(8,128)(2,1)}, bf16[8,64,128]{2,1,0:T(8,128)(2,1)S(1)}, u32[]{:S(2)}, u32[]{:S(2)}) collective-permute-start(bf16[8,64,128]{2,1,0:T(8,128)(2,1)} %bitcast.17), channel_id=1, source_target_pairs={{0,1},{1,0},{2,3},{3,2},{4,5},{5,4},{6,7},{7,6},{8,9},{9,8},{10,11... | collective-permute-start | bytes 393224 | tf_op jit(solution)/shard_map/ppermute | solution.py:18
  3.6 6.0 %copy-start.5 = (s32[1,1152]{1,0:T(1,128)S(1)}, s32[1,1152]{1,0:T(1,128)}, u32[]{:S(2)}) copy-start(s32[1,1152]{1,0:T(1,128)} %param.21) | copy-start | bytes 13828
  3.6 6.1 %copy-start.1 = (bf16[1,2,1152,192]{2,3,1,0:T(8,128)(2,1)S(1)}, bf16[1,2,1152,192]{2,3,1,0:T(8,128)(2,1)}, u32[]{:S(2)}) copy-start(bf16[1,2,1152,192]{2,3,1,0:T(8,128)(2,1)} %param.24) | copy-start | bytes 2654212
  3.6 6.1 %copy-start.4 = (s32[1,2]{1,0:T(1,128)S(1)}, s32[1,2]{1,0:T(1,128)}, u32[]{:S(2)}) copy-start(s32[1,2]{1,0:T(1,128)} %near.1) | copy-start | bytes 28
  5.5 7.4 %collective-permute-start.1 = (bf16[64,768]{1,0:T(8,128)(2,1)S(1)}, bf16[64,768]{1,0:T(8,128)(2,1)S(1)}, u32[]{:S(2)}, u32[]{:S(2)}) collective-permute-start(bf16[64,768]{1,0:T(8,128)(2,1)S(1)} %get-tuple-element.28), channel_id=1, source_target_pairs={{0,2},{1,0},{2,4},{3,1},{4,6},{5,3},{6,8},{7,5},{8,10},{9,7},{10,1... | collective-permute-start | bytes 294920 | tf_op jit(solution)/shard_map/ppermute | solution.py:32
  7.0 7.5 %collective-permute-start.2 = (bf16[64,768]{1,0:T(8,128)(2,1)S(1)}, bf16[64,768]{1,0:T(8,128)(2,1)S(1)}, u32[]{:S(2)}, u32[]{:S(2)}) collective-permute-start(bf16[64,768]{1,0:T(8,128)(2,1)S(1)} %get-tuple-element.29), channel_id=1, source_target_pairs={{0,1},{1,3},{2,0},{3,5},{4,2},{5,7},{6,4},{7,9},{8,6},{9,11},{10,8... | collective-permute-start | bytes 294920 | tf_op jit(solution)/shard_map/ppermute | solution.py:32
  7.6 9.0 %collective-permute-start.3 = (bf16[64,768]{1,0:T(8,128)(2,1)S(1)}, bf16[64,768]{1,0:T(8,128)(2,1)S(1)}, u32[]{:S(2)}, u32[]{:S(2)}) collective-permute-start(bf16[64,768]{1,0:T(8,128)(2,1)S(1)} %get-tuple-element.30), channel_id=1, source_target_pairs={{0,4},{1,0},{2,6},{3,2},{4,8},{5,1},{6,10},{7,3},{8,12},{9,5},{10,... | collective-permute-start | bytes 294920 | tf_op jit(solution)/shard_map/ppermute | solution.py:32
  9.1 7.4 %collective-permute-start.4 = (bf16[64,768]{1,0:T(8,128)(2,1)S(1)}, bf16[64,768]{1,0:T(8,128)(2,1)S(1)}, u32[]{:S(2)}, u32[]{:S(2)}) collective-permute-start(bf16[64,768]{1,0:T(8,128)(2,1)S(1)} %get-tuple-element.31), channel_id=1, source_target_pairs={{0,1},{1,5},{2,3},{3,7},{4,0},{5,9},{6,2},{7,11},{8,4},{9,13},{10,... | collective-permute-start | bytes 294920 | tf_op jit(solution)/shard_map/ppermute | solution.py:32
  9.7 10.7 %copy-start.6 = (s32[1,384]{1,0:T(1,128)S(1)}, s32[1,384]{1,0:T(1,128)}, u32[]{:S(2)}) copy-start(s32[1,384]{1,0:T(1,128)} %param.20) | copy-start | bytes 4612
  9.7 10.8 %copy-start = (bf16[1,1152,576]{1,2,0:T(8,128)(2,1)S(1)}, bf16[1,1152,576]{1,2,0:T(8,128)(2,1)}, u32[]{:S(2)}) copy-start(bf16[1,1152,576]{1,2,0:T(8,128)(2,1)} %param.23) | copy-start | bytes 3981316
  9.7 10.8 %copy-start.2 = (bf16[1,1152,192]{1,2,0:T(8,128)(2,1)S(1)}, bf16[1,1152,192]{1,2,0:T(8,128)(2,1)}, u32[]{:S(2)}) copy-start(bf16[1,1152,192]{1,2,0:T(8,128)(2,1)} %param.22) | copy-start | bytes 1327108
  16.6 1.4 %collective-permute-start.5 = (bf16[64,768]{1,0:T(8,128)(2,1)S(1)}, bf16[64,768]{1,0:T(8,128)(2,1)S(1)}, u32[]{:S(2)}, u32[]{:S(2)}) collective-permute-start(bf16[64,768]{1,0:T(8,128)(2,1)S(1)} %shard_map.151.refs_0_), channel_id=1, source_target_pairs={{0,1},{1,0},{2,3},{3,2},{4,5},{5,4},{6,7},{7,6},{8,9},{9,8},{10,11... | collective-permute-start | bytes 294920 | tf_op jit(solution)/shard_map/ppermute | solution.py:18
  18.4 4.1 %collective-permute-start.6 = (bf16[64,192]{1,0:T(8,128)(2,1)S(1)}, bf16[64,192]{1,0:T(8,128)(2,1)S(1)}, u32[]{:S(2)}, u32[]{:S(2)}) collective-permute-start(bf16[64,192]{1,0:T(8,128)(2,1)S(1)} %get-tuple-element.35), channel_id=1, source_target_pairs={{0,2},{1,0},{2,4},{3,1},{4,6},{5,3},{6,8},{7,5},{8,10},{9,7},{10,1... | collective-permute-start | bytes 73736 | tf_op jit(solution)/shard_map/ppermute | solution.py:32
  20.4 5.7 %collective-permute-start.7 = (bf16[64,192]{1,0:T(8,128)(2,1)S(1)}, bf16[64,192]{1,0:T(8,128)(2,1)S(1)}, u32[]{:S(2)}, u32[]{:S(2)}) collective-permute-start(bf16[64,192]{1,0:T(8,128)(2,1)S(1)} %get-tuple-element.36), channel_id=1, source_target_pairs={{0,1},{1,3},{2,0},{3,5},{4,2},{5,7},{6,4},{7,9},{8,6},{9,11},{10,8... | collective-permute-start | bytes 73736 | tf_op jit(solution)/shard_map/ppermute | solution.py:32

commit v3 on v2

v3 whole, which is shorter than its diff:
```python
import functools

import jax
import jax.numpy as jnp
from jax import lax
from jax.experimental import pallas as pl
from jax.experimental.pallas import tpu as pltpu
from jax.sharding import PartitionSpec as P

F32 = jnp.float32
BF16 = jnp.bfloat16
REACH = 2


def row_pieces(block):
    rows = lax.axis_size("row")
    others = [
        lax.ppermute(block, "row", [(i, i ^ t) for i in range(rows)]) for t in range(1, rows)
    ]
    return [block] + others


def goes_up(box, distance, flip):
    return ((box // distance) % 2 == 0) != flip


def box_permute(block, distance, flip):
    boxes, rows = lax.axis_size("box"), lax.axis_size("row")
    route = []
    for box in range(boxes):
        target = box + (distance if goes_up(box, distance, flip) else -distance)
        inside = 0 <= target < boxes
        for row in range(rows):
            place = target * rows + row if inside else box * rows + (row ^ 1)
            route.append((box * rows + row, place))
    return lax.ppermute(block, ("box", "row"), route)


def onehot(index, count, dtype=BF16):
    spots = lax.broadcasted_iota(jnp.int32, (count, index.shape[1]), 0)
    return jnp.where(spots == index, 1.0, 0.0).astype(dtype)


def dot(a, b):
    return jnp.dot(a, b, preferred_element_type=F32)


def dot_t(a, b):
    return lax.dot_general(a, b, (((1,), (1,)), ((), ())), preferred_element_type=F32)


def turned(panel):
    return jnp.swapaxes(panel, -1, -2)


def own_part(values, block):
    row = lax.axis_index("row")
    chosen = values[:, :block]
    for place in range(1, values.shape[1] // block):
        part = values[:, place * block : (place + 1) * block]
        chosen = jnp.where(row == place, part, chosen)
    return chosen


def struct(shape, dtype):
    return jax.ShapeDtypeStruct(shape, dtype)


def pick_kernel(
    red, rhs, near, couple, inv,
    xr_out, rhs_out, near_out, couple_out, inv_out, red_in, spots, sems,
):
    groups, _, total = rhs.shape
    pairs = [(red, red_in)] + [(rhs.at[g], rhs_out.at[g]) for g in range(groups)]
    pairs += [(near, near_out), (inv, inv_out)]
    block = couple.shape[2]
    pairs += [(couple.at[g], couple_out.at[g, :, :block, :]) for g in range(groups)]
    copies = [
        pltpu.make_async_copy(source, held, sems.at[i]) for i, (source, held) in enumerate(pairs)
    ]
    for copy in copies:
        copy.start()
    copies[0].wait()
    for g in range(groups):
        spots[g] = onehot(red_in[g : g + 1, :], total)
    for copy in copies[1 : groups + 1]:
        copy.wait()
    for g in range(groups):
        xr_out[g] = dot(rhs_out[g].astype(BF16), spots[g]).astype(BF16)
    for copy in copies[groups + 1 :]:
        copy.wait()


def leaf_kernel(rows, block, near_held, xr, *refs):
    inv = refs[:rows]
    couple, own_out = refs[rows : rows + 2]
    sends = refs[rows + 2 : rows + 2 + len(ROUTES)]
    acc, near, sem = refs[-3:]
    fetch = pltpu.make_async_copy(near_held, near, sem)
    fetch.start()
    groups, slots = near.shape
    lanes = couple.shape[2]
    row = lax.axis_index("row")
    anchor = lax.axis_index("box")
    acc[...] = jnp.zeros_like(acc)
    leaves = []
    for g in range(groups):
        parts = [dot_t(xr[g], inv[t][g]) for t in range(rows)]
        placed = []
        for place in range(rows):
            chosen = parts[0]
            for t in range(1, rows):
                chosen = jnp.where(row == (place ^ t), parts[t], chosen)
            placed.append(chosen)
        leaves.append(jnp.concatenate(placed, axis=1).astype(BF16))
    fetch.wait()
    for g in range(groups):
        updates = dot_t(leaves[g], couple[g].reshape(slots * lanes, couple.shape[3]))
        for j in range(slots):
            target = near[g, j]
            clear = target - (anchor - REACH) * groups
            spot = jnp.where(target >= 0, clear, acc.shape[0] - 1)
            acc[spot] += updates[:, j * lanes : j * lanes + block]

    def merged(section):
        first = (section + REACH) * groups
        return jnp.concatenate([acc[first + g] for g in range(groups)], axis=1)

    own_out[...] = merged(0)
    for send, (distance, flip) in zip(sends, ROUTES):
        section = jnp.where(goes_up(anchor, distance, flip), distance, -distance)
        send[...] = merged(section).astype(BF16)


ROUTES = ((2, False), (1, True), (2, True), (1, False))


def shifted_index(index, half, block, groups, skeletons):
    child, place = index // skeletons, index % skeletons
    piece = (place // block) ^ half
    return piece * (groups * block) + child * block + place % block


def spread_kernel(near, red, panel, xr, inv1, rhs, skel, interp, red_out, ys_out, out):
    groups, columns, total = rhs.shape
    block = interp.shape[1]
    own = own_part(skel[...], block)
    for g in range(groups):
        red_out[g] = dot_t(xr[g], inv1[g])
        whole = rhs[g]
        high = whole.astype(BF16)
        low = (whole - high.astype(F32)).astype(BF16)
        both = dot(jnp.concatenate([high, low], axis=0), onehot(own[g : g + 1, :], total))
        ys = both[:columns] + both[columns:] - dot_t(xr[g], interp[g])
        ys_out[:, g * block : (g + 1) * block] = ys
    spots = onehot(red[...], out.shape[1])
    for slot in range(out.shape[0]):
        spread = dot_t(spots, panel[0, slot])
        out[slot] = jnp.where(near[0, slot] >= 0, spread, 0.0).astype(BF16)


def sum_kernel(own, *refs):
    total = own[...]
    for ref in refs[:-1]:
        total = total + ref[...].astype(F32)
    refs[-1][...] = total.astype(BF16)


def update_kernel(panel, *refs):
    pieces, sends = refs[:-2], refs[-2:]
    parent = jnp.concatenate([piece[...] for piece in pieces], axis=1)
    for send, flip in zip(sends, (True, False)):
        slot = jnp.where(goes_up(lax.axis_index("box"), 1, flip), 1, 0)
        send[...] = dot(parent, panel[slot]).astype(BF16)


def finish_kernel(red, skel, inv, interp, *refs):
    pieces, (red_out, ys_out) = refs[:-2], refs[-2:]
    parent = jnp.concatenate([piece[...] for piece in pieces], axis=1)
    count = parent.shape[1]
    xr = dot(parent, onehot(red[...], count)).astype(BF16)
    red_out[0] = dot_t(xr, inv[0])
    ys_out[0] = dot(parent, onehot(skel[...], count)) - dot_t(xr, interp[0])


def shards(
    rhs, skel1, red1, interp1, inv1, couple1, near1, skel2, red2, interp2, inv2, panel2, near2
):
    rows = lax.axis_size("row")
    row = lax.axis_index("row")
    groups, columns, total = rhs.shape
    redundant, block = interp1.shape[1:]
    skeletons = skel1.shape[1]
    width = groups * block
    s2_block, i2_block = interp2.shape[2], inv2.shape[2]
    red2_count = red2.shape[1]

    inverse = row_pieces(turned(inv1))[1:]
    vmem = pl.BlockSpec(memory_space=pltpu.VMEM)
    smem = pl.BlockSpec(memory_space=pltpu.SMEM)
    hbm = pl.BlockSpec(memory_space=pltpu.HBM)
    params = pltpu.CompilerParams(vmem_limit_bytes=48 << 20)
    inv1, couple1 = turned(inv1), turned(couple1)
    held = [pltpu.with_memory_space_constraint(v, pltpu.HBM) for v in (red1, rhs, near1, couple1, inv1)]
    lanes = -(-block // 128) * 128
    shapes = [v.shape for v in held[1:]]
    shapes[2] = shapes[2][:2] + (lanes, shapes[2][3])
    xr1, rhs, near1, couple1, own_inv1 = pl.pallas_call(
        pick_kernel,
        out_shape=(struct((groups, columns, redundant), BF16),)
        + tuple(struct(shape, v.dtype) for shape, v in zip(shapes, held[1:])),
        in_specs=[hbm] * 5,
        scratch_shapes=[
            pltpu.VMEM(red1.shape, jnp.int32),
            pltpu.VMEM((groups, total, redundant), BF16),
            pltpu.SemaphoreType.DMA((2 * groups + 3,)),
        ],
        compiler_params=params,
    )(*held)

    send = struct((columns, width), BF16)
    own, *sends = pl.pallas_call(
        functools.partial(leaf_kernel, rows, block),
        out_shape=(struct((columns, width), F32),) + (send,) * len(ROUTES),
        in_specs=[vmem] * (rows + 3),
        scratch_shapes=[
            pltpu.VMEM(((2 * REACH + 1) * groups + 1, columns, block), F32),
            pltpu.SMEM(near1.shape, jnp.int32),
            pltpu.SemaphoreType.DMA,
        ],
        compiler_params=params,
    )(near1, xr1, own_inv1, *inverse, couple1)

    arrived = [
        box_permute(piece, distance, flip) for piece, (distance, flip) in zip(sends, ROUTES)
    ]

    place2 = functools.partial(
        shifted_index, half=row, block=block, groups=groups, skeletons=skeletons
    )
    red_place, skel_place = place2(red2), place2(
        lax.dynamic_slice_in_dim(skel2, row * s2_block, s2_block, 1)
    )
    red_one, ys1, panel_spread = pl.pallas_call(
        spread_kernel,
        out_shape=(
            struct((groups, columns, inv1.shape[1]), F32),
            struct((columns, width), F32),
            struct((near2.shape[1], rows * width, s2_block), BF16),
        ),
        in_specs=[smem] + [vmem] * 7,
        compiler_params=params,
    )(near2, red_place, turned(panel2), xr1, own_inv1, rhs, skel1, turned(interp1))
    high = pl.pallas_call(sum_kernel, out_shape=send, compiler_params=params)(own, ys1, *arrived)
    pieces = row_pieces(high)
    updates = pl.pallas_call(
        update_kernel,
        out_shape=(struct((columns, s2_block), BF16),) * 2,
        compiler_params=params,
    )(panel_spread, *pieces)
    moved = [box_permute(piece, 1, flip) for piece, flip in zip(updates, (True, False))]
    red_two, ys2 = pl.pallas_call(
        finish_kernel,
        out_shape=(struct((1, columns, i2_block), F32), struct((1, columns, s2_block), F32)),
        compiler_params=params,
    )(red_place, skel_place, turned(inv2), turned(interp2), *pieces)
    skel_two = ys2 + moved[0].astype(F32)[None] + moved[1].astype(F32)[None]
    return red_one, red_two, skel_two


def solution(mesh):
    return jax.shard_map(
        shards,
        mesh=mesh,
        in_specs=(
            P("box", None, None),
            P("box", None),
            P("box", None),
            P("box", None, "row"),
            P("box", None, "row"),
            P("box", None, None, "row"),
            P("box", None),
            P("box", None),
            P("box", None),
            P("box", None, "row"),
            P("box", None, "row"),
            P("box", None, None, "row"),
            P("box", None),
        ),
        out_specs=(P("box", None, "row"), P("box", None, "row"), P("box", None, "row")),
        check_vma=False,
    )
```

time: 26.9 us -> 23.3 us (0.87)
  the two profiles are of different devices: /device:TPU:6 before, /device:TPU:24 now
where the time goes in v3:
time: 23.3 us; the launch traced here: 23.1 us
  Pallas kernels  9.86 us (42%)
  starting transfers between devices  8.2 us (35%)
  waiting for transfers between devices  3.41 us (15%)
  other arithmetic  0.82 us (4%)
  between operations  0.79 us (3%)
    ppermute x6, starting transfers between devices, box_permute(): return lax.ppermute(block, ('box', 'row'), route)  8.06 us
    pallas_call x1, Pallas kernels, shards(): pl.pallas_call(spread_kernel, out_shape=(struct((groups, columns, inv1.sh...  3.87 us
    ppermute x6, waiting for transfers between devices, box_permute(): return lax.ppermute(block, ('box', 'row'), route)  2.12 us
    pallas_call x1, Pallas kernels, shards(): pl.pallas_call(pick_kernel, out_shape=(struct((groups, columns, redundant...  1.92 us
    pallas_call x1, Pallas kernels, shards(): pl.pallas_call(finish_kernel, out_shape=(struct((1, columns, i2_block), F...  1.91 us
    pallas_call x1, Pallas kernels, shards(): pl.pallas_call(functools.partial(leaf_kernel, rows, block), out_shape=(st...  1.71 us
    ppermute x2, waiting for transfers between devices, row_pieces(): lax.ppermute(block, 'row', [(i, i ^ t) for i in range(rows)])  1.29 us
    add x1, other arithmetic, shards(): skel_two = ys2 + moved[0].astype(F32)[None] + moved[1].astype(F32)[None]  0.64 us
  transfers between devices with their start and end apart: 8, of which 4 were waited for; matrix products, arithmetic and copies ran while one was open for 1% of the time, Pallas kernels for 33%

profile of v3, /device:TPU:24, one launch (start us, length us, event | category | flops | bytes accessed | tf_op | source)
XLA Modules:
  0.0 23.1 jit_solution(4801691143448641790)
XLA Ops:
  0.6 0.1 collective-permute-start
  0.7 1.9 %shard_map.148 = (bf16[8,64,128]{2,1,0:T(8,128)(2,1)S(1)}, f32[8,64,320]{2,1,0:T(8,128)S(1)}, s32[8,8]{1,0:T(8,128)S(1)}, bf16[8,8,128,128]{3,2,1,0:T(8,128)(2,1)S(1)}, bf16[8,64,128]{2,1,0:T(8,128)(2,1)S(1)}) custom-call(s32[8,128]{1,0:T(8,128)} %red.1, f32[8,64,320]{2,1,0:T(8,128)} %rhs.1, s32[8,8]{1,0:T(8,128)} %near.2, bf16[8,8,96,128]{3,2,1,0:T(8,128)(2,1)} %bitcast.16, ...), custom_call_target="tpu_custom_call" | custom-call | tf_op jit(solution)/shard_map/pallas_call | solution.py:208
  2.6 0.0 copy-start.6
  2.7 0.0 copy-start.1
  2.7 0.0 copy-start.3
  2.7 0.0 copy-start.4
  2.7 0.0 copy-start.5
  2.7 0.0 collective-permute-done.refs_1_
  2.7 1.7 %shard_map.150 = (f32[64,768]{1,0:T(8,128)S(1)}, bf16[64,768]{1,0:T(8,128)(2,1)S(1)}, bf16[64,768]{1,0:T(8,128)(2,1)S(1)}, bf16[64,768]{1,0:T(8,128)(2,1)S(1)}, bf16[64,768]{1,0:T(8,128)(2,1)S(1)}) custom-call(s32[8,8]{1,0:T(8,128)S(1)} %get-tuple-element.24.near_held, bf16[8,64,128]{2,1,0:T(8,128)(2,1)S(1)} %get-tuple-element.20.xr, ...), custom_call_target="tpu_custom_call" | custom-call | tf_op jit(solution)/shard_map/pallas_call | solution.py:222
  4.4 1.6 %collective-permute-start.1 = (bf16[64,768]{1,0:T(8,128)(2,1)S(1)}, bf16[64,768]{1,0:T(8,128)(2,1)S(1)}, u32[]{:S(2)}, u32[]{:S(2)}) collective-permute-start(bf16[64,768]{1,0:T(8,128)(2,1)S(1)} %get-tuple-element.28), channel_id=1, source_target_pairs={{0,4},{1,5},{2,6},{3,7},{4,0},{5,1},{6,2},{7,3},{8,12},{9,13},{10,... | collective-permute-start | bytes 294920 | tf_op jit(solution)/shard_map/ppermute | solution.py:36
  6.0 1.3 %collective-permute-start.2 = (bf16[64,768]{1,0:T(8,128)(2,1)S(1)}, bf16[64,768]{1,0:T(8,128)(2,1)S(1)}, u32[]{:S(2)}, u32[]{:S(2)}) collective-permute-start(bf16[64,768]{1,0:T(8,128)(2,1)S(1)} %get-tuple-element.29), channel_id=1, source_target_pairs={{0,1},{1,0},{2,4},{3,5},{4,2},{5,3},{6,8},{7,9},{8,6},{9,7},{10,12... | collective-permute-start | bytes 294920 | tf_op jit(solution)/shard_map/ppermute | solution.py:36
  7.3 1.5 %collective-permute-start.3 = (bf16[64,768]{1,0:T(8,128)(2,1)S(1)}, bf16[64,768]{1,0:T(8,128)(2,1)S(1)}, u32[]{:S(2)}, u32[]{:S(2)}) collective-permute-start(bf16[64,768]{1,0:T(8,128)(2,1)S(1)} %get-tuple-element.30), channel_id=1, source_target_pairs={{0,1},{1,0},{2,3},{3,2},{4,8},{5,9},{6,10},{7,11},{8,4},{9,5},{10,... | collective-permute-start | bytes 294920 | tf_op jit(solution)/shard_map/ppermute | solution.py:36
  8.8 1.6 %collective-permute-start.4 = (bf16[64,768]{1,0:T(8,128)(2,1)S(1)}, bf16[64,768]{1,0:T(8,128)(2,1)S(1)}, u32[]{:S(2)}, u32[]{:S(2)}) collective-permute-start(bf16[64,768]{1,0:T(8,128)(2,1)S(1)} %get-tuple-element.31), channel_id=1, source_target_pairs={{0,2},{1,3},{2,0},{3,1},{4,6},{5,7},{6,4},{7,5},{8,10},{9,11},{10,... | collective-permute-start | bytes 294920 | tf_op jit(solution)/shard_map/ppermute | solution.py:36
  10.4 0.0 copy-done.6
  10.4 0.1 fusion.red
  10.5 0.0 copy-done.1
  10.5 0.0 copy-done.3
  10.5 0.0 copy-done.4
  10.5 0.0 copy-done.5
  10.5 3.9 %shard_map.149 = (f32[8,64,64]{2,1,0:T(8,128)}, f32[64,768]{1,0:T(8,128)S(1)}, bf16[2,1536,192]{2,1,0:T(8,128)(2,1)S(1)}) custom-call(s32[1,2]{1,0:T(1,128)S(1)} %copy-done.5, s32[1,1152]{1,0:T(1,128)S(1)} %fusion.red, bf16[1,2,192,1152]{3,2,1,0:T(8,128)(2,1)S(1)} %bitcast.13, bf16[8,64,128]{2,1,0:T(8,128)(2,1)S(1)} %get-tuple-element.20.xr, ...), custom_call_target="tpu_custom_call" | custom-call | tf_op jit(solution)/shard_map/pallas_call | solution.py:244
  14.4 0.0 copy-start.7
  14.4 0.0 copy-start
  14.4 0.0 copy-start.2
  14.4 0.0 collective-permute-done.1.refs_1_
  14.4 0.2 collective-permute-done.2.refs_2_
  14.6 0.2 collective-permute-done.3.refs_3_
  14.8 0.0 collective-permute-done.4.refs_4_
  14.8 0.1 shard_map.151.refs_0_
  14.9 0.1 collective-permute-start.5
  15.0 1.3 %collective-permute-done.5.refs_1_ = bf16[64,768]{1,0:T(8,128)(2,1)S(1)} collective-permute-done((bf16[64,768]{1,0:T(8,128)(2,1)S(1)}, bf16[64,768]{1,0:T(8,128)(2,1)S(1)}, u32[]{:S(2)}, u32[]{:S(2)}) %collective-permute-start.5) | collective-permute-done | bytes 98336 | tf_op jit(solution)/shard_map/ppermute | solution.py:18
  16.3 0.4 %shard_map.153 = (bf16[64,192]{1,0:T(8,128)(2,1)S(1)}, bf16[64,192]{1,0:T(8,128)(2,1)S(1)}) custom-call(bf16[2,1536,192]{2,1,0:T(8,128)(2,1)S(1)} %get-tuple-element.34.panel, bf16[64,768]{1,0:T(8,128)(2,1)S(1)} %shard_map.151.refs_0_, bf16[64,768]{1,0:T(8,128)(2,1)S(1)} %collective-permute-done.5.refs_1_), custom_call_target="tpu_custom_call" | custom-call | tf_op jit(solution)/shard_map/pallas_call | solution.py:256
  16.7 1.5 %collective-permute-start.6 = (bf16[64,192]{1,0:T(8,128)(2,1)S(1)}, bf16[64,192]{1,0:T(8,128)(2,1)S(1)}, u32[]{:S(2)}, u32[]{:S(2)}) collective-permute-start(bf16[64,192]{1,0:T(8,128)(2,1)S(1)} %get-tuple-element.35), channel_id=1, source_target_pairs={{0,1},{1,0},{2,4},{3,5},{4,2},{5,3},{6,8},{7,9},{8,6},{9,7},{10,12... | collective-permute-start | bytes 73736 | tf_op jit(solution)/shard_map/ppermute | solution.py:36
  18.1 0.6 %collective-permute-start.7 = (bf16[64,192]{1,0:T(8,128)(2,1)S(1)}, bf16[64,192]{1,0:T(8,128)(2,1)S(1)}, u32[]{:S(2)}, u32[]{:S(2)}) collective-permute-start(bf16[64,192]{1,0:T(8,128)(2,1)S(1)} %get-tuple-element.36), channel_id=1, source_target_pairs={{0,2},{1,3},{2,0},{3,1},{4,6},{5,7},{6,4},{7,5},{8,10},{9,11},{10,... | collective-permute-start | bytes 73736 | tf_op jit(solution)/shard_map/ppermute | solution.py:36
  18.8 0.0 copy-done.7
  18.8 0.1 fusion.1.skel
  18.9 0.0 copy-done
  18.9 0.0 copy-done.2
  18.9 1.9 %shard_map.152 = (f32[1,64,576]{2,1,0:T(8,128)}, f32[1,64,192]{2,1,0:T(8,128)S(1)}) custom-call(s32[1,1152]{1,0:T(1,128)S(1)} %fusion.red, s32[1,192]{1,0:T(1,128)S(1)} %fusion.1.skel, bf16[1,576,1152]{2,1,0:T(8,128)(2,1)S(1)} %bitcast.12, bf16[1,192,1152]{2,1,0:T(8,128)(2,1)S(1)} %bitcast.14, bf16[64,768]{1,0:T(8,128)(2,1)S(1)} %shard_map.151.refs_0_, ...), custom_call_target="tpu_custom_call" | custom-call | tf_op jit(solution)/shard_map/pallas_call | solution.py:262
  20.8 1.7 %collective-permute-done.6 = bf16[64,192]{1,0:T(8,128)(2,1)S(1)} collective-permute-done((bf16[64,192]{1,0:T(8,128)(2,1)S(1)}, bf16[64,192]{1,0:T(8,128)(2,1)S(1)}, u32[]{:S(2)}, u32[]{:S(2)}) %collective-permute-start.6) | collective-permute-done | bytes 24608 | tf_op jit(solution)/shard_map/ppermute | solution.py:36
  22.5 0.0 collective-permute-done.7
  22.5 0.6 %convert_add_fusion = f32[1,64,192]{2,1,0:T(8,128)} fusion(f32[1,64,192]{2,1,0:T(8,128)S(1)} %get-tuple-element.33, bf16[64,192]{1,0:T(8,128)(2,1)S(1)} %collective-permute-done.7, bf16[64,192]{1,0:T(8,128)(2,1)S(1)} %collective-permute-done.6), kind=kLoop, calls=%fused_computation | loop fusion | flops 49152 | bytes 147456 | tf_op jit(solution)/shard_map/add | solution.py:267
Async XLA Ops:
  0.6 2.1 %collective-permute-start = (bf16[8,64,128]{2,1,0:T(8,128)(2,1)}, bf16[8,64,128]{2,1,0:T(8,128)(2,1)S(1)}, u32[]{:S(2)}, u32[]{:S(2)}) collective-permute-start(bf16[8,64,128]{2,1,0:T(8,128)(2,1)} %bitcast.17), channel_id=1, source_target_pairs={{0,1},{1,0},{2,3},{3,2},{4,5},{5,4},{6,7},{7,6},{8,9},{9,8},{10,11... | collective-permute-start | bytes 393224 | tf_op jit(solution)/shard_map/ppermute | solution.py:18
  2.6 7.8 %copy-start.6 = (s32[1,1152]{1,0:T(1,128)S(1)}, s32[1,1152]{1,0:T(1,128)}, u32[]{:S(2)}) copy-start(s32[1,1152]{1,0:T(1,128)} %param.21) | copy-start | bytes 13828
  2.7 7.8 %copy-start.1 = (bf16[1,2,1152,192]{2,3,1,0:T(8,128)(2,1)S(1)}, bf16[1,2,1152,192]{2,3,1,0:T(8,128)(2,1)}, u32[]{:S(2)}) copy-start(bf16[1,2,1152,192]{2,3,1,0:T(8,128)(2,1)} %param.24) | copy-start | bytes 2654212
  2.7 7.8 %copy-start.3 = (bf16[8,128,96]{1,2,0:T(8,128)(2,1)S(1)}, bf16[8,128,96]{1,2,0:T(8,128)(2,1)}, u32[]{:S(2)}) copy-start(bf16[8,128,96]{1,2,0:T(8,128)(2,1)} %param.16) | copy-start | bytes 589828
  2.7 7.8 %copy-start.4 = (s32[8,192]{1,0:T(8,128)S(1)}, s32[8,192]{1,0:T(8,128)}, u32[]{:S(2)}) copy-start(s32[8,192]{1,0:T(8,128)} %skel.1) | copy-start | bytes 18436
  2.7 7.8 %copy-start.5 = (s32[1,2]{1,0:T(1,128)S(1)}, s32[1,2]{1,0:T(1,128)}, u32[]{:S(2)}) copy-start(s32[1,2]{1,0:T(1,128)} %near.3) | copy-start | bytes 28
  4.4 10.0 %collective-permute-start.1 = (bf16[64,768]{1,0:T(8,128)(2,1)S(1)}, bf16[64,768]{1,0:T(8,128)(2,1)S(1)}, u32[]{:S(2)}, u32[]{:S(2)}) collective-permute-start(bf16[64,768]{1,0:T(8,128)(2,1)S(1)} %get-tuple-element.28), channel_id=1, source_target_pairs={{0,4},{1,5},{2,6},{3,7},{4,0},{5,1},{6,2},{7,3},{8,12},{9,13},{10,... | collective-permute-start | bytes 294920 | tf_op jit(solution)/shard_map/ppermute | solution.py:36
  6.0 8.6 %collective-permute-start.2 = (bf16[64,768]{1,0:T(8,128)(2,1)S(1)}, bf16[64,768]{1,0:T(8,128)(2,1)S(1)}, u32[]{:S(2)}, u32[]{:S(2)}) collective-permute-start(bf16[64,768]{1,0:T(8,128)(2,1)S(1)} %get-tuple-element.29), channel_id=1, source_target_pairs={{0,1},{1,0},{2,4},{3,5},{4,2},{5,3},{6,8},{7,9},{8,6},{9,7},{10,12... | collective-permute-start | bytes 294920 | tf_op jit(solution)/shard_map/ppermute | solution.py:36
  7.3 7.5 %collective-permute-start.3 = (bf16[64,768]{1,0:T(8,128)(2,1)S(1)}, bf16[64,768]{1,0:T(8,128)(2,1)S(1)}, u32[]{:S(2)}, u32[]{:S(2)}) collective-permute-start(bf16[64,768]{1,0:T(8,128)(2,1)S(1)} %get-tuple-element.30), channel_id=1, source_target_pairs={{0,1},{1,0},{2,3},{3,2},{4,8},{5,9},{6,10},{7,11},{8,4},{9,5},{10,... | collective-permute-start | bytes 294920 | tf_op jit(solution)/shard_map/ppermute | solution.py:36
  8.8 6.0 %collective-permute-start.4 = (bf16[64,768]{1,0:T(8,128)(2,1)S(1)}, bf16[64,768]{1,0:T(8,128)(2,1)S(1)}, u32[]{:S(2)}, u32[]{:S(2)}) collective-permute-start(bf16[64,768]{1,0:T(8,128)(2,1)S(1)} %get-tuple-element.31), channel_id=1, source_target_pairs={{0,2},{1,3},{2,0},{3,1},{4,6},{5,7},{6,4},{7,5},{8,10},{9,11},{10,... | collective-permute-start | bytes 294920 | tf_op jit(solution)/shard_map/ppermute | solution.py:36
  14.4 4.4 %copy-start.7 = (s32[1,384]{1,0:T(1,128)S(1)}, s32[1,384]{1,0:T(1,128)}, u32[]{:S(2)}) copy-start(s32[1,384]{1,0:T(1,128)} %param.20) | copy-start | bytes 4612
  14.4 4.5 %copy-start = (bf16[1,1152,576]{1,2,0:T(8,128)(2,1)S(1)}, bf16[1,1152,576]{1,2,0:T(8,128)(2,1)}, u32[]{:S(2)}) copy-start(bf16[1,1152,576]{1,2,0:T(8,128)(2,1)} %param.23) | copy-start | bytes 3981316
  14.4 4.5 %copy-start.2 = (bf16[1,1152,192]{1,2,0:T(8,128)(2,1)S(1)}, bf16[1,1152,192]{1,2,0:T(8,128)(2,1)}, u32[]{:S(2)}) copy-start(bf16[1,1152,192]{1,2,0:T(8,128)(2,1)} %param.22) | copy-start | bytes 1327108
  14.9 1.4 %collective-permute-start.5 = (bf16[64,768]{1,0:T(8,128)(2,1)S(1)}, bf16[64,768]{1,0:T(8,128)(2,1)S(1)}, u32[]{:S(2)}, u32[]{:S(2)}) collective-permute-start(bf16[64,768]{1,0:T(8,128)(2,1)S(1)} %shard_map.151.refs_0_), channel_id=1, source_target_pairs={{0,1},{1,0},{2,3},{3,2},{4,5},{5,4},{6,7},{7,6},{8,9},{9,8},{10,11... | collective-permute-start | bytes 294920 | tf_op jit(solution)/shard_map/ppermute | solution.py:18
  16.7 5.8 %collective-permute-start.6 = (bf16[64,192]{1,0:T(8,128)(2,1)S(1)}, bf16[64,192]{1,0:T(8,128)(2,1)S(1)}, u32[]{:S(2)}, u32[]{:S(2)}) collective-permute-start(bf16[64,192]{1,0:T(8,128)(2,1)S(1)} %get-tuple-element.35), channel_id=1, source_target_pairs={{0,1},{1,0},{2,4},{3,5},{4,2},{5,3},{6,8},{7,9},{8,6},{9,7},{10,12... | collective-permute-start | bytes 73736 | tf_op jit(solution)/shard_map/ppermute | solution.py:36
  18.1 4.4 %collective-permute-start.7 = (bf16[64,192]{1,0:T(8,128)(2,1)S(1)}, bf16[64,192]{1,0:T(8,128)(2,1)S(1)}, u32[]{:S(2)}, u32[]{:S(2)}) collective-permute-start(bf16[64,192]{1,0:T(8,128)(2,1)S(1)} %get-tuple-element.36), channel_id=1, source_target_pairs={{0,2},{1,3},{2,0},{3,1},{4,6},{5,7},{6,4},{7,5},{8,10},{9,11},{10,... | collective-permute-start | bytes 73736 | tf_op jit(solution)/shard_map/ppermute | solution.py:36

commit v4 on v3

--- a/solution.py
+++ b/solution.py
@@ -202,7 +202,7 @@
     params = pltpu.CompilerParams(vmem_limit_bytes=48 << 20)
     inv1, couple1 = turned(inv1), turned(couple1)
     held = [pltpu.with_memory_space_constraint(v, pltpu.HBM) for v in (red1, rhs, near1, couple1, inv1)]
-    lanes = -(-block // 128) * 128
+    lanes = -(-block // 128) * 128 if block % 16 == 0 else block
     shapes = [v.shape for v in held[1:]]
     shapes[2] = shapes[2][:2] + (lanes, shapes[2][3])
     xr1, rhs, near1, couple1, own_inv1 = pl.pallas_call(

time: 23.3 us -> 23.3 us (level)
  no operation moved by 1% of the time
where the time goes in v4:
time: 23.3 us; the launch traced here: 23.1 us
  Pallas kernels  9.87 us (42%)
  starting transfers between devices  8.19 us (35%)
  waiting for transfers between devices  3.42 us (15%)
  other arithmetic  0.82 us (4%)
  between operations  0.79 us (3%)
    ppermute x6, starting transfers between devices, box_permute(): return lax.ppermute(block, ('box', 'row'), route)  8.05 us
    pallas_call x1, Pallas kernels, shards(): pl.pallas_call(spread_kernel, out_shape=(struct((groups, columns, inv1.sh...  3.87 us
    ppermute x6, waiting for transfers between devices, box_permute(): return lax.ppermute(block, ('box', 'row'), route)  2.13 us
    pallas_call x1, Pallas kernels, shards(): pl.pallas_call(pick_kernel, out_shape=(struct((groups, columns, redundant...  1.92 us
    pallas_call x1, Pallas kernels, shards(): pl.pallas_call(finish_kernel, out_shape=(struct((1, columns, i2_block), F...  1.91 us
    pallas_call x1, Pallas kernels, shards(): pl.pallas_call(functools.partial(leaf_kernel, rows, block), out_shape=(st...  1.71 us
    ppermute x2, waiting for transfers between devices, row_pieces(): lax.ppermute(block, 'row', [(i, i ^ t) for i in range(rows)])  1.29 us
    add x1, other arithmetic, shards(): skel_two = ys2 + moved[0].astype(F32)[None] + moved[1].astype(F32)[None]  0.64 us
  transfers between devices with their start and end apart: 8, of which 4 were waited for; matrix products, arithmetic and copies ran while one was open for 1% of the time, Pallas kernels for 33%

profile of v4, /device:TPU:24, one launch (start us, length us, event | category | flops | bytes accessed | tf_op | source)
XLA Modules:
  0.0 23.1 jit_solution(4801691143448641790)
XLA Ops:
  0.6 0.1 collective-permute-start
  0.7 1.9 %shard_map.148 = (bf16[8,64,128]{2,1,0:T(8,128)(2,1)S(1)}, f32[8,64,320]{2,1,0:T(8,128)S(1)}, s32[8,8]{1,0:T(8,128)S(1)}, bf16[8,8,128,128]{3,2,1,0:T(8,128)(2,1)S(1)}, bf16[8,64,128]{2,1,0:T(8,128)(2,1)S(1)}) custom-call(s32[8,128]{1,0:T(8,128)} %red.1, f32[8,64,320]{2,1,0:T(8,128)} %rhs.1, s32[8,8]{1,0:T(8,128)} %near.2, bf16[8,8,96,128]{3,2,1,0:T(8,128)(2,1)} %bitcast.16, ...), custom_call_target="tpu_custom_call" | custom-call | tf_op jit(solution)/shard_map/pallas_call | solution.py:208
  2.6 0.0 copy-start.6
  2.7 0.0 copy-start.1
  2.7 0.0 copy-start.3
  2.7 0.0 copy-start.4
  2.7 0.0 copy-start.5
  2.7 0.0 collective-permute-done.refs_1_
  2.7 1.7 %shard_map.150 = (f32[64,768]{1,0:T(8,128)S(1)}, bf16[64,768]{1,0:T(8,128)(2,1)S(1)}, bf16[64,768]{1,0:T(8,128)(2,1)S(1)}, bf16[64,768]{1,0:T(8,128)(2,1)S(1)}, bf16[64,768]{1,0:T(8,128)(2,1)S(1)}) custom-call(s32[8,8]{1,0:T(8,128)S(1)} %get-tuple-element.24.near_held, bf16[8,64,128]{2,1,0:T(8,128)(2,1)S(1)} %get-tuple-element.20.xr, ...), custom_call_target="tpu_custom_call" | custom-call | tf_op jit(solution)/shard_map/pallas_call | solution.py:222
  4.4 1.6 %collective-permute-start.1 = (bf16[64,768]{1,0:T(8,128)(2,1)S(1)}, bf16[64,768]{1,0:T(8,128)(2,1)S(1)}, u32[]{:S(2)}, u32[]{:S(2)}) collective-permute-start(bf16[64,768]{1,0:T(8,128)(2,1)S(1)} %get-tuple-element.28), channel_id=1, source_target_pairs={{0,4},{1,5},{2,6},{3,7},{4,0},{5,1},{6,2},{7,3},{8,12},{9,13},{10,... | collective-permute-start | bytes 294920 | tf_op jit(solution)/shard_map/ppermute | solution.py:36
  6.0 1.3 %collective-permute-start.2 = (bf16[64,768]{1,0:T(8,128)(2,1)S(1)}, bf16[64,768]{1,0:T(8,128)(2,1)S(1)}, u32[]{:S(2)}, u32[]{:S(2)}) collective-permute-start(bf16[64,768]{1,0:T(8,128)(2,1)S(1)} %get-tuple-element.29), channel_id=1, source_target_pairs={{0,1},{1,0},{2,4},{3,5},{4,2},{5,3},{6,8},{7,9},{8,6},{9,7},{10,12... | collective-permute-start | bytes 294920 | tf_op jit(solution)/shard_map/ppermute | solution.py:36
  7.3 1.5 %collective-permute-start.3 = (bf16[64,768]{1,0:T(8,128)(2,1)S(1)}, bf16[64,768]{1,0:T(8,128)(2,1)S(1)}, u32[]{:S(2)}, u32[]{:S(2)}) collective-permute-start(bf16[64,768]{1,0:T(8,128)(2,1)S(1)} %get-tuple-element.30), channel_id=1, source_target_pairs={{0,1},{1,0},{2,3},{3,2},{4,8},{5,9},{6,10},{7,11},{8,4},{9,5},{10,... | collective-permute-start | bytes 294920 | tf_op jit(solution)/shard_map/ppermute | solution.py:36
  8.8 1.5 %collective-permute-start.4 = (bf16[64,768]{1,0:T(8,128)(2,1)S(1)}, bf16[64,768]{1,0:T(8,128)(2,1)S(1)}, u32[]{:S(2)}, u32[]{:S(2)}) collective-permute-start(bf16[64,768]{1,0:T(8,128)(2,1)S(1)} %get-tuple-element.31), channel_id=1, source_target_pairs={{0,2},{1,3},{2,0},{3,1},{4,6},{5,7},{6,4},{7,5},{8,10},{9,11},{10,... | collective-permute-start | bytes 294920 | tf_op jit(solution)/shard_map/ppermute | solution.py:36
  10.4 0.0 copy-done.6
  10.4 0.1 fusion.red
  10.5 0.0 copy-done.1
  10.5 0.0 copy-done.3
  10.5 0.0 copy-done.4
  10.5 0.0 copy-done.5
  10.5 3.9 %shard_map.149 = (f32[8,64,64]{2,1,0:T(8,128)}, f32[64,768]{1,0:T(8,128)S(1)}, bf16[2,1536,192]{2,1,0:T(8,128)(2,1)S(1)}) custom-call(s32[1,2]{1,0:T(1,128)S(1)} %copy-done.5, s32[1,1152]{1,0:T(1,128)S(1)} %fusion.red, bf16[1,2,192,1152]{3,2,1,0:T(8,128)(2,1)S(1)} %bitcast.13, bf16[8,64,128]{2,1,0:T(8,128)(2,1)S(1)} %get-tuple-element.20.xr, ...), custom_call_target="tpu_custom_call" | custom-call | tf_op jit(solution)/shard_map/pallas_call | solution.py:244
  14.4 0.0 copy-start.7
  14.4 0.0 copy-start
  14.4 0.0 copy-start.2
  14.4 0.0 collective-permute-done.1.refs_1_
  14.4 0.2 collective-permute-done.2.refs_2_
  14.6 0.2 collective-permute-done.3.refs_3_
  14.8 0.0 collective-permute-done.4.refs_4_
  14.8 0.1 shard_map.151.refs_0_
  14.9 0.1 collective-permute-start.5
  15.0 1.3 %collective-permute-done.5.refs_1_ = bf16[64,768]{1,0:T(8,128)(2,1)S(1)} collective-permute-done((bf16[64,768]{1,0:T(8,128)(2,1)S(1)}, bf16[64,768]{1,0:T(8,128)(2,1)S(1)}, u32[]{:S(2)}, u32[]{:S(2)}) %collective-permute-start.5) | collective-permute-done | bytes 98336 | tf_op jit(solution)/shard_map/ppermute | solution.py:18
  16.3 0.4 %shard_map.153 = (bf16[64,192]{1,0:T(8,128)(2,1)S(1)}, bf16[64,192]{1,0:T(8,128)(2,1)S(1)}) custom-call(bf16[2,1536,192]{2,1,0:T(8,128)(2,1)S(1)} %get-tuple-element.34.panel, bf16[64,768]{1,0:T(8,128)(2,1)S(1)} %shard_map.151.refs_0_, bf16[64,768]{1,0:T(8,128)(2,1)S(1)} %collective-permute-done.5.refs_1_), custom_call_target="tpu_custom_call" | custom-call | tf_op jit(solution)/shard_map/pallas_call | solution.py:256
  16.7 1.5 %collective-permute-start.6 = (bf16[64,192]{1,0:T(8,128)(2,1)S(1)}, bf16[64,192]{1,0:T(8,128)(2,1)S(1)}, u32[]{:S(2)}, u32[]{:S(2)}) collective-permute-start(bf16[64,192]{1,0:T(8,128)(2,1)S(1)} %get-tuple-element.35), channel_id=1, source_target_pairs={{0,1},{1,0},{2,4},{3,5},{4,2},{5,3},{6,8},{7,9},{8,6},{9,7},{10,12... | collective-permute-start | bytes 73736 | tf_op jit(solution)/shard_map/ppermute | solution.py:36
  18.1 0.6 %collective-permute-start.7 = (bf16[64,192]{1,0:T(8,128)(2,1)S(1)}, bf16[64,192]{1,0:T(8,128)(2,1)S(1)}, u32[]{:S(2)}, u32[]{:S(2)}) collective-permute-start(bf16[64,192]{1,0:T(8,128)(2,1)S(1)} %get-tuple-element.36), channel_id=1, source_target_pairs={{0,2},{1,3},{2,0},{3,1},{4,6},{5,7},{6,4},{7,5},{8,10},{9,11},{10,... | collective-permute-start | bytes 73736 | tf_op jit(solution)/shard_map/ppermute | solution.py:36
  18.8 0.0 copy-done.7
  18.8 0.1 fusion.1.skel
  18.9 0.0 copy-done
  18.9 0.0 copy-done.2
  18.9 1.9 %shard_map.152 = (f32[1,64,576]{2,1,0:T(8,128)}, f32[1,64,192]{2,1,0:T(8,128)S(1)}) custom-call(s32[1,1152]{1,0:T(1,128)S(1)} %fusion.red, s32[1,192]{1,0:T(1,128)S(1)} %fusion.1.skel, bf16[1,576,1152]{2,1,0:T(8,128)(2,1)S(1)} %bitcast.12, bf16[1,192,1152]{2,1,0:T(8,128)(2,1)S(1)} %bitcast.14, bf16[64,768]{1,0:T(8,128)(2,1)S(1)} %shard_map.151.refs_0_, ...), custom_call_target="tpu_custom_call" | custom-call | tf_op jit(solution)/shard_map/pallas_call | solution.py:262
  20.8 1.7 %collective-permute-done.6 = bf16[64,192]{1,0:T(8,128)(2,1)S(1)} collective-permute-done((bf16[64,192]{1,0:T(8,128)(2,1)S(1)}, bf16[64,192]{1,0:T(8,128)(2,1)S(1)}, u32[]{:S(2)}, u32[]{:S(2)}) %collective-permute-start.6) | collective-permute-done | bytes 24608 | tf_op jit(solution)/shard_map/ppermute | solution.py:36
  22.5 0.0 collective-permute-done.7
  22.5 0.6 %convert_add_fusion = f32[1,64,192]{2,1,0:T(8,128)} fusion(f32[1,64,192]{2,1,0:T(8,128)S(1)} %get-tuple-element.33, bf16[64,192]{1,0:T(8,128)(2,1)S(1)} %collective-permute-done.7, bf16[64,192]{1,0:T(8,128)(2,1)S(1)} %collective-permute-done.6), kind=kLoop, calls=%fused_computation | loop fusion | flops 49152 | bytes 147456 | tf_op jit(solution)/shard_map/add | solution.py:267
Async XLA Ops:
  0.6 2.1 %collective-permute-start = (bf16[8,64,128]{2,1,0:T(8,128)(2,1)}, bf16[8,64,128]{2,1,0:T(8,128)(2,1)S(1)}, u32[]{:S(2)}, u32[]{:S(2)}) collective-permute-start(bf16[8,64,128]{2,1,0:T(8,128)(2,1)} %bitcast.17), channel_id=1, source_target_pairs={{0,1},{1,0},{2,3},{3,2},{4,5},{5,4},{6,7},{7,6},{8,9},{9,8},{10,11... | collective-permute-start | bytes 393224 | tf_op jit(solution)/shard_map/ppermute | solution.py:18
  2.6 7.8 %copy-start.6 = (s32[1,1152]{1,0:T(1,128)S(1)}, s32[1,1152]{1,0:T(1,128)}, u32[]{:S(2)}) copy-start(s32[1,1152]{1,0:T(1,128)} %param.21) | copy-start | bytes 13828
  2.7 7.8 %copy-start.1 = (bf16[1,2,1152,192]{2,3,1,0:T(8,128)(2,1)S(1)}, bf16[1,2,1152,192]{2,3,1,0:T(8,128)(2,1)}, u32[]{:S(2)}) copy-start(bf16[1,2,1152,192]{2,3,1,0:T(8,128)(2,1)} %param.24) | copy-start | bytes 2654212
  2.7 7.8 %copy-start.3 = (bf16[8,128,96]{1,2,0:T(8,128)(2,1)S(1)}, bf16[8,128,96]{1,2,0:T(8,128)(2,1)}, u32[]{:S(2)}) copy-start(bf16[8,128,96]{1,2,0:T(8,128)(2,1)} %param.16) | copy-start | bytes 589828
  2.7 7.8 %copy-start.4 = (s32[8,192]{1,0:T(8,128)S(1)}, s32[8,192]{1,0:T(8,128)}, u32[]{:S(2)}) copy-start(s32[8,192]{1,0:T(8,128)} %skel.1) | copy-start | bytes 18436
  2.7 7.8 %copy-start.5 = (s32[1,2]{1,0:T(1,128)S(1)}, s32[1,2]{1,0:T(1,128)}, u32[]{:S(2)}) copy-start(s32[1,2]{1,0:T(1,128)} %near.3) | copy-start | bytes 28
  4.4 10.0 %collective-permute-start.1 = (bf16[64,768]{1,0:T(8,128)(2,1)S(1)}, bf16[64,768]{1,0:T(8,128)(2,1)S(1)}, u32[]{:S(2)}, u32[]{:S(2)}) collective-permute-start(bf16[64,768]{1,0:T(8,128)(2,1)S(1)} %get-tuple-element.28), channel_id=1, source_target_pairs={{0,4},{1,5},{2,6},{3,7},{4,0},{5,1},{6,2},{7,3},{8,12},{9,13},{10,... | collective-permute-start | bytes 294920 | tf_op jit(solution)/shard_map/ppermute | solution.py:36
  6.0 8.6 %collective-permute-start.2 = (bf16[64,768]{1,0:T(8,128)(2,1)S(1)}, bf16[64,768]{1,0:T(8,128)(2,1)S(1)}, u32[]{:S(2)}, u32[]{:S(2)}) collective-permute-start(bf16[64,768]{1,0:T(8,128)(2,1)S(1)} %get-tuple-element.29), channel_id=1, source_target_pairs={{0,1},{1,0},{2,4},{3,5},{4,2},{5,3},{6,8},{7,9},{8,6},{9,7},{10,12... | collective-permute-start | bytes 294920 | tf_op jit(solution)/shard_map/ppermute | solution.py:36
  7.3 7.5 %collective-permute-start.3 = (bf16[64,768]{1,0:T(8,128)(2,1)S(1)}, bf16[64,768]{1,0:T(8,128)(2,1)S(1)}, u32[]{:S(2)}, u32[]{:S(2)}) collective-permute-start(bf16[64,768]{1,0:T(8,128)(2,1)S(1)} %get-tuple-element.30), channel_id=1, source_target_pairs={{0,1},{1,0},{2,3},{3,2},{4,8},{5,9},{6,10},{7,11},{8,4},{9,5},{10,... | collective-permute-start | bytes 294920 | tf_op jit(solution)/shard_map/ppermute | solution.py:36
  8.8 6.0 %collective-permute-start.4 = (bf16[64,768]{1,0:T(8,128)(2,1)S(1)}, bf16[64,768]{1,0:T(8,128)(2,1)S(1)}, u32[]{:S(2)}, u32[]{:S(2)}) collective-permute-start(bf16[64,768]{1,0:T(8,128)(2,1)S(1)} %get-tuple-element.31), channel_id=1, source_target_pairs={{0,2},{1,3},{2,0},{3,1},{4,6},{5,7},{6,4},{7,5},{8,10},{9,11},{10,... | collective-permute-start | bytes 294920 | tf_op jit(solution)/shard_map/ppermute | solution.py:36
  14.4 4.4 %copy-start.7 = (s32[1,384]{1,0:T(1,128)S(1)}, s32[1,384]{1,0:T(1,128)}, u32[]{:S(2)}) copy-start(s32[1,384]{1,0:T(1,128)} %param.20) | copy-start | bytes 4612
  14.4 4.5 %copy-start = (bf16[1,1152,576]{1,2,0:T(8,128)(2,1)S(1)}, bf16[1,1152,576]{1,2,0:T(8,128)(2,1)}, u32[]{:S(2)}) copy-start(bf16[1,1152,576]{1,2,0:T(8,128)(2,1)} %param.23) | copy-start | bytes 3981316
  14.4 4.5 %copy-start.2 = (bf16[1,1152,192]{1,2,0:T(8,128)(2,1)S(1)}, bf16[1,1152,192]{1,2,0:T(8,128)(2,1)}, u32[]{:S(2)}) copy-start(bf16[1,1152,192]{1,2,0:T(8,128)(2,1)} %param.22) | copy-start | bytes 1327108
  14.9 1.4 %collective-permute-start.5 = (bf16[64,768]{1,0:T(8,128)(2,1)S(1)}, bf16[64,768]{1,0:T(8,128)(2,1)S(1)}, u32[]{:S(2)}, u32[]{:S(2)}) collective-permute-start(bf16[64,768]{1,0:T(8,128)(2,1)S(1)} %shard_map.151.refs_0_), channel_id=1, source_target_pairs={{0,1},{1,0},{2,3},{3,2},{4,5},{5,4},{6,7},{7,6},{8,9},{9,8},{10,11... | collective-permute-start | bytes 294920 | tf_op jit(solution)/shard_map/ppermute | solution.py:18
  16.7 5.8 %collective-permute-start.6 = (bf16[64,192]{1,0:T(8,128)(2,1)S(1)}, bf16[64,192]{1,0:T(8,128)(2,1)S(1)}, u32[]{:S(2)}, u32[]{:S(2)}) collective-permute-start(bf16[64,192]{1,0:T(8,128)(2,1)S(1)} %get-tuple-element.35), channel_id=1, source_target_pairs={{0,1},{1,0},{2,4},{3,5},{4,2},{5,3},{6,8},{7,9},{8,6},{9,7},{10,12... | collective-permute-start | bytes 73736 | tf_op jit(solution)/shard_map/ppermute | solution.py:36
  18.1 4.4 %collective-permute-start.7 = (bf16[64,192]{1,0:T(8,128)(2,1)S(1)}, bf16[64,192]{1,0:T(8,128)(2,1)S(1)}, u32[]{:S(2)}, u32[]{:S(2)}) collective-permute-start(bf16[64,192]{1,0:T(8,128)(2,1)S(1)} %get-tuple-element.36), channel_id=1, source_target_pairs={{0,2},{1,3},{2,0},{3,1},{4,6},{5,7},{6,4},{7,5},{8,10},{9,11},{10,... | collective-permute-start | bytes 73736 | tf_op jit(solution)/shard_map/ppermute | solution.py:36

commit v5 on v4

--- a/solution.py
+++ b/solution.py
@@ -113,9 +113,11 @@
                 chosen = jnp.where(row == (place ^ t), parts[t], chosen)
             placed.append(chosen)
         leaves.append(jnp.concatenate(placed, axis=1).astype(BF16))
+    products = [
+        dot_t(leaves[g], couple[g].reshape(slots * lanes, couple.shape[3])) for g in range(groups)
+    ]
     fetch.wait()
-    for g in range(groups):
-        updates = dot_t(leaves[g], couple[g].reshape(slots * lanes, couple.shape[3]))
+    for g, updates in enumerate(products):
         for j in range(slots):
             target = near[g, j]
             clear = target - (anchor - REACH) * groups
@@ -167,11 +169,18 @@
 
 
 def update_kernel(panel, *refs):
-    pieces, sends = refs[:-2], refs[-2:]
+    pieces, first, sends = refs[:-4], refs[-4:-2], refs[-2:]
+    width = pieces[0].shape[1]
     parent = jnp.concatenate([piece[...] for piece in pieces], axis=1)
+    for begun, send, flip in zip(first, sends, (True, False)):
+        slot = jnp.where(goes_up(lax.axis_index("box"), 1, flip), 1, 0)
+        send[...] = (begun[...] + dot(parent, panel[slot, width:])).astype(BF16)
+
+
+def own_update_kernel(panel, piece, *sends):
     for send, flip in zip(sends, (True, False)):
         slot = jnp.where(goes_up(lax.axis_index("box"), 1, flip), 1, 0)
-        send[...] = dot(parent, panel[slot]).astype(BF16)
+        send[...] = dot(piece[...], panel[slot, : piece.shape[1]])
 
 
 def finish_kernel(red, skel, inv, interp, *refs):
@@ -231,6 +240,9 @@
         compiler_params=params,
     )(near1, xr1, own_inv1, *inverse, couple1)
 
+    panel2, inv2, interp2, interp1, skel1, red2, skel2, near2, _ = lax.optimization_barrier(
+        (panel2, inv2, interp2, interp1, skel1, red2, skel2, near2, sends[0])
+    )
     arrived = [
         box_permute(piece, distance, flip) for piece, (distance, flip) in zip(sends, ROUTES)
     ]
@@ -253,11 +265,16 @@
     )(near2, red_place, turned(panel2), xr1, own_inv1, rhs, skel1, turned(interp1))
     high = pl.pallas_call(sum_kernel, out_shape=send, compiler_params=params)(own, ys1, *arrived)
     pieces = row_pieces(high)
+    begun = pl.pallas_call(
+        own_update_kernel,
+        out_shape=(struct((columns, s2_block), F32),) * 2,
+        compiler_params=params,
+    )(panel_spread, pieces[0])
     updates = pl.pallas_call(
         update_kernel,
         out_shape=(struct((columns, s2_block), BF16),) * 2,
         compiler_params=params,
-    )(panel_spread, *pieces)
+    )(panel_spread, *pieces[1:], *begun)
     moved = [box_permute(piece, 1, flip) for piece, flip in zip(updates, (True, False))]
     red_two, ys2 = pl.pallas_call(
         finish_kernel,

time: 23.3 us -> 23.2 us (level)
  waiting for transfers between devices: 3.42 us -> 3.13 us
    ppermute x2, waiting for transfers between devices: 1.29 us -> 0.98 us  [row_pieces(): lax.ppermute(block, 'row', [(i, i ^ t) for i in range(rows)])]
    pallas_call x0 -> x1, Pallas kernels: none -> 0.27 us  [shards(): pl.pallas_call(own_update_kernel, out_shape=(struct((columns, s2_block),...]
  transfers between devices with their start and end apart: 8 -> 8, of which waited for: 4 -> 4; matrix products, arithmetic and copies ran while one was open for 1% -> 1% of each run, Pallas kernels for 33% -> 35%
where the time goes in v5:
time: 23.2 us; the launch traced here: 23 us
  Pallas kernels  9.99 us (43%)
  starting transfers between devices  8.2 us (35%)
  waiting for transfers between devices  3.13 us (13%)
  other arithmetic  0.83 us (4%)
  between operations  0.8 us (3%)
    ppermute x6, starting transfers between devices, box_permute(): return lax.ppermute(block, ('box', 'row'), route)  8.06 us
    pallas_call x1, Pallas kernels, shards(): pl.pallas_call(spread_kernel, out_shape=(struct((groups, columns, inv1.sh...  3.86 us
    ppermute x6, waiting for transfers between devices, box_permute(): return lax.ppermute(block, ('box', 'row'), route)  2.15 us
    pallas_call x1, Pallas kernels, shards(): pl.pallas_call(pick_kernel, out_shape=(struct((groups, columns, redundant...  1.92 us
    pallas_call x1, Pallas kernels, shards(): pl.pallas_call(finish_kernel, out_shape=(struct((1, columns, i2_block), F...  1.91 us
    pallas_call x1, Pallas kernels, shards(): pl.pallas_call(functools.partial(leaf_kernel, rows, block), out_shape=(st...  1.7 us
    ppermute x2, waiting for transfers between devices, row_pieces(): lax.ppermute(block, 'row', [(i, i ^ t) for i in range(rows)])  0.98 us
    add x1, other arithmetic, shards(): skel_two = ys2 + moved[0].astype(F32)[None] + moved[1].astype(F32)[None]  0.64 us
  transfers between devices with their start and end apart: 8, of which 4 were waited for; matrix products, arithmetic and copies ran while one was open for 1% of the time, Pallas kernels for 35%

profile of v5, /device:TPU:24, one launch (start us, length us, event | category | flops | bytes accessed | tf_op | source)
XLA Modules:
  0.0 23.0 jit_solution(16258017485492335105)
XLA Ops:
  0.6 0.1 collective-permute-start
  0.7 1.9 %shard_map.148 = (bf16[8,64,128]{2,1,0:T(8,128)(2,1)S(1)}, f32[8,64,320]{2,1,0:T(8,128)S(1)}, s32[8,8]{1,0:T(8,128)S(1)}, bf16[8,8,128,128]{3,2,1,0:T(8,128)(2,1)S(1)}, bf16[8,64,128]{2,1,0:T(8,128)(2,1)S(1)}) custom-call(s32[8,128]{1,0:T(8,128)} %red.1, f32[8,64,320]{2,1,0:T(8,128)} %rhs.1, s32[8,8]{1,0:T(8,128)} %near.1, bf16[8,8,96,128]{3,2,1,0:T(8,128)(2,1)} %bitcast.16, ...), custom_call_target="tpu_custom_call" | custom-call | tf_op jit(solution)/shard_map/pallas_call | solution.py:217
  2.6 0.0 copy-start.6
  2.7 0.0 copy-start.1
  2.7 0.0 copy-start.3
  2.7 0.0 copy-start.4
  2.7 0.0 copy-start.5
  2.7 0.0 collective-permute-done.refs_1_
  2.7 1.7 %shard_map.149 = (f32[64,768]{1,0:T(8,128)S(1)}, bf16[64,768]{1,0:T(8,128)(2,1)S(1)}, bf16[64,768]{1,0:T(8,128)(2,1)S(1)}, bf16[64,768]{1,0:T(8,128)(2,1)S(1)}, bf16[64,768]{1,0:T(8,128)(2,1)S(1)}) custom-call(s32[8,8]{1,0:T(8,128)S(1)} %get-tuple-element.30.near_held, bf16[8,64,128]{2,1,0:T(8,128)(2,1)S(1)} %get-tuple-element.31.xr, ...), custom_call_target="tpu_custom_call" | custom-call | tf_op jit(solution)/shard_map/pallas_call | solution.py:231
  4.4 1.6 %collective-permute-start.1 = (bf16[64,768]{1,0:T(8,128)(2,1)S(1)}, bf16[64,768]{1,0:T(8,128)(2,1)S(1)}, u32[]{:S(2)}, u32[]{:S(2)}) collective-permute-start(bf16[64,768]{1,0:T(8,128)(2,1)S(1)} %get-tuple-element.34), channel_id=1, source_target_pairs={{0,4},{1,5},{2,6},{3,7},{4,0},{5,1},{6,2},{7,3},{8,12},{9,13},{10,... | collective-permute-start | bytes 294920 | tf_op jit(solution)/shard_map/ppermute | solution.py:36
  6.0 1.3 %collective-permute-start.2 = (bf16[64,768]{1,0:T(8,128)(2,1)S(1)}, bf16[64,768]{1,0:T(8,128)(2,1)S(1)}, u32[]{:S(2)}, u32[]{:S(2)}) collective-permute-start(bf16[64,768]{1,0:T(8,128)(2,1)S(1)} %get-tuple-element.47), channel_id=1, source_target_pairs={{0,1},{1,0},{2,4},{3,5},{4,2},{5,3},{6,8},{7,9},{8,6},{9,7},{10,12... | collective-permute-start | bytes 294920 | tf_op jit(solution)/shard_map/ppermute | solution.py:36
  7.3 1.5 %collective-permute-start.3 = (bf16[64,768]{1,0:T(8,128)(2,1)S(1)}, bf16[64,768]{1,0:T(8,128)(2,1)S(1)}, u32[]{:S(2)}, u32[]{:S(2)}) collective-permute-start(bf16[64,768]{1,0:T(8,128)(2,1)S(1)} %get-tuple-element.48), channel_id=1, source_target_pairs={{0,1},{1,0},{2,3},{3,2},{4,8},{5,9},{6,10},{7,11},{8,4},{9,5},{10,... | collective-permute-start | bytes 294920 | tf_op jit(solution)/shard_map/ppermute | solution.py:36
  8.8 1.6 %collective-permute-start.4 = (bf16[64,768]{1,0:T(8,128)(2,1)S(1)}, bf16[64,768]{1,0:T(8,128)(2,1)S(1)}, u32[]{:S(2)}, u32[]{:S(2)}) collective-permute-start(bf16[64,768]{1,0:T(8,128)(2,1)S(1)} %get-tuple-element.49), channel_id=1, source_target_pairs={{0,2},{1,3},{2,0},{3,1},{4,6},{5,7},{6,4},{7,5},{8,10},{9,11},{10,... | collective-permute-start | bytes 294920 | tf_op jit(solution)/shard_map/ppermute | solution.py:36
  10.4 0.0 copy-done.6
  10.4 0.1 fusion.red
  10.5 0.0 copy-done.1
  10.5 0.0 copy-done.3
  10.5 0.0 copy-done.4
  10.5 0.0 copy-done.5
  10.5 3.9 %shard_map.150 = (f32[8,64,64]{2,1,0:T(8,128)}, f32[64,768]{1,0:T(8,128)S(1)}, bf16[2,1536,192]{2,1,0:T(8,128)(2,1)S(1)}) custom-call(s32[1,2]{1,0:T(1,128)S(1)} %copy-done.5, s32[1,1152]{1,0:T(1,128)S(1)} %fusion.red, bf16[1,2,192,1152]{3,2,1,0:T(8,128)(2,1)S(1)} %bitcast.13, bf16[8,64,128]{2,1,0:T(8,128)(2,1)S(1)} %get-tuple-element.31.xr, ...), custom_call_target="tpu_custom_call" | custom-call | tf_op jit(solution)/shard_map/pallas_call | solution.py:256
  14.4 0.0 collective-permute-done.1.refs_1_
  14.4 0.2 %collective-permute-done.2.refs_2_ = bf16[64,768]{1,0:T(8,128)(2,1)S(1)} collective-permute-done((bf16[64,768]{1,0:T(8,128)(2,1)S(1)}, bf16[64,768]{1,0:T(8,128)(2,1)S(1)}, u32[]{:S(2)}, u32[]{:S(2)}) %collective-permute-start.2) | collective-permute-done | bytes 98336 | tf_op jit(solution)/shard_map/ppermute | solution.py:36
  14.6 0.2 collective-permute-done.3.refs_3_
  14.8 0.0 collective-permute-done.4.refs_4_
  14.8 0.1 shard_map.151.refs_0_.piece
  14.9 0.1 collective-permute-start.5
  15.0 0.0 copy-start.7
  15.0 0.0 copy-start
  15.0 0.0 copy-start.2
  15.0 0.3 %shard_map.153 = (f32[64,192]{1,0:T(8,128)S(1)}, f32[64,192]{1,0:T(8,128)S(1)}) custom-call(bf16[2,1536,192]{2,1,0:T(8,128)(2,1)S(1)} %get-tuple-element.52.panel, bf16[64,768]{1,0:T(8,128)(2,1)S(1)} %shard_map.151.refs_0_.piece), custom_call_target="tpu_custom_call" | custom-call | tf_op jit(solution)/shard_map/pallas_call | solution.py:268
  15.3 1.0 %collective-permute-done.5.refs_1_.refs_0_ = bf16[64,768]{1,0:T(8,128)(2,1)S(1)} collective-permute-done((bf16[64,768]{1,0:T(8,128)(2,1)S(1)}, bf16[64,768]{1,0:T(8,128)(2,1)S(1)}, u32[]{:S(2)}, u32[]{:S(2)}) %collective-permute-start.5) | collective-permute-done | bytes 98336 | tf_op jit(solution)/shard_map/ppermute | solution.py:18
  16.3 0.3 %shard_map.154 = (bf16[64,192]{1,0:T(8,128)(2,1)S(1)}, bf16[64,192]{1,0:T(8,128)(2,1)S(1)}) custom-call(bf16[2,1536,192]{2,1,0:T(8,128)(2,1)S(1)} %get-tuple-element.52.panel, bf16[64,768]{1,0:T(8,128)(2,1)S(1)} %collective-permute-done.5.refs_1_.refs_0_, f32[64,192]{1,0:T(8,128)S(1)} %get-tuple-element.53.refs_1_, f32[64,192]{1,0:T(8,128)S(1)} %get-tuple-element.54.refs_2_), custom_call_target="tpu_custom_call" | custom-call | tf_op jit(solution)/shard_map/pallas_call | solution.py:273
  16.5 1.5 %collective-permute-start.6 = (bf16[64,192]{1,0:T(8,128)(2,1)S(1)}, bf16[64,192]{1,0:T(8,128)(2,1)S(1)}, u32[]{:S(2)}, u32[]{:S(2)}) collective-permute-start(bf16[64,192]{1,0:T(8,128)(2,1)S(1)} %get-tuple-element.55), channel_id=1, source_target_pairs={{0,1},{1,0},{2,4},{3,5},{4,2},{5,3},{6,8},{7,9},{8,6},{9,7},{10,12... | collective-permute-start | bytes 73736 | tf_op jit(solution)/shard_map/ppermute | solution.py:36
  18.0 0.6 %collective-permute-start.7 = (bf16[64,192]{1,0:T(8,128)(2,1)S(1)}, bf16[64,192]{1,0:T(8,128)(2,1)S(1)}, u32[]{:S(2)}, u32[]{:S(2)}) collective-permute-start(bf16[64,192]{1,0:T(8,128)(2,1)S(1)} %get-tuple-element.56), channel_id=1, source_target_pairs={{0,2},{1,3},{2,0},{3,1},{4,6},{5,7},{6,4},{7,5},{8,10},{9,11},{10,... | collective-permute-start | bytes 73736 | tf_op jit(solution)/shard_map/ppermute | solution.py:36
  18.6 0.0 copy-done.7
  18.6 0.1 fusion.1.skel
  18.7 0.0 copy-done
  18.7 0.0 copy-done.2
  18.7 1.9 %shard_map.152 = (f32[1,64,576]{2,1,0:T(8,128)}, f32[1,64,192]{2,1,0:T(8,128)S(1)}) custom-call(s32[1,1152]{1,0:T(1,128)S(1)} %fusion.red, s32[1,192]{1,0:T(1,128)S(1)} %fusion.1.skel, bf16[1,576,1152]{2,1,0:T(8,128)(2,1)S(1)} %bitcast.12, bf16[1,192,1152]{2,1,0:T(8,128)(2,1)S(1)} %bitcast.14, bf16[64,768]{1,0:T(8,128)(2,1)S(1)} %shard_map.151.refs_0_.piece, ...), custom_call_target="tpu_custom_call" | custom-call | tf_op jit(solution)/shard_map/pallas_call | solution.py:279
  20.6 1.7 %collective-permute-done.6 = bf16[64,192]{1,0:T(8,128)(2,1)S(1)} collective-permute-done((bf16[64,192]{1,0:T(8,128)(2,1)S(1)}, bf16[64,192]{1,0:T(8,128)(2,1)S(1)}, u32[]{:S(2)}, u32[]{:S(2)}) %collective-permute-start.6) | collective-permute-done | bytes 24608 | tf_op jit(solution)/shard_map/ppermute | solution.py:36
  22.4 0.0 collective-permute-done.7
  22.4 0.6 %convert_add_fusion = f32[1,64,192]{2,1,0:T(8,128)} fusion(f32[1,64,192]{2,1,0:T(8,128)S(1)} %get-tuple-element.51, bf16[64,192]{1,0:T(8,128)(2,1)S(1)} %collective-permute-done.7, bf16[64,192]{1,0:T(8,128)(2,1)S(1)} %collective-permute-done.6), kind=kLoop, calls=%fused_computation | loop fusion | flops 49152 | bytes 147456 | tf_op jit(solution)/shard_map/add | solution.py:284
Async XLA Ops:
  0.6 2.1 %collective-permute-start = (bf16[8,64,128]{2,1,0:T(8,128)(2,1)}, bf16[8,64,128]{2,1,0:T(8,128)(2,1)S(1)}, u32[]{:S(2)}, u32[]{:S(2)}) collective-permute-start(bf16[8,64,128]{2,1,0:T(8,128)(2,1)} %bitcast.17), channel_id=1, source_target_pairs={{0,1},{1,0},{2,3},{3,2},{4,5},{5,4},{6,7},{7,6},{8,9},{9,8},{10,11... | collective-permute-start | bytes 393224 | tf_op jit(solution)/shard_map/ppermute | solution.py:18
  2.6 7.8 %copy-start.6 = (s32[1,1152]{1,0:T(1,128)S(1)}, s32[1,1152]{1,0:T(1,128)}, u32[]{:S(2)}) copy-start(s32[1,1152]{1,0:T(1,128)} %param.21) | copy-start | bytes 13828
  2.7 7.8 %copy-start.1 = (bf16[1,2,1152,192]{2,3,1,0:T(8,128)(2,1)S(1)}, bf16[1,2,1152,192]{2,3,1,0:T(8,128)(2,1)}, u32[]{:S(2)}) copy-start(bf16[1,2,1152,192]{2,3,1,0:T(8,128)(2,1)} %param.24) | copy-start | bytes 2654212
  2.7 7.8 %copy-start.3 = (bf16[8,128,96]{1,2,0:T(8,128)(2,1)S(1)}, bf16[8,128,96]{1,2,0:T(8,128)(2,1)}, u32[]{:S(2)}) copy-start(bf16[8,128,96]{1,2,0:T(8,128)(2,1)} %param.16) | copy-start | bytes 589828
  2.7 7.8 %copy-start.4 = (s32[8,192]{1,0:T(8,128)S(1)}, s32[8,192]{1,0:T(8,128)}, u32[]{:S(2)}) copy-start(s32[8,192]{1,0:T(8,128)} %skel) | copy-start | bytes 18436
  2.7 7.8 %copy-start.5 = (s32[1,2]{1,0:T(1,128)S(1)}, s32[1,2]{1,0:T(1,128)}, u32[]{:S(2)}) copy-start(s32[1,2]{1,0:T(1,128)} %near.2) | copy-start | bytes 28
  4.4 10.0 %collective-permute-start.1 = (bf16[64,768]{1,0:T(8,128)(2,1)S(1)}, bf16[64,768]{1,0:T(8,128)(2,1)S(1)}, u32[]{:S(2)}, u32[]{:S(2)}) collective-permute-start(bf16[64,768]{1,0:T(8,128)(2,1)S(1)} %get-tuple-element.34), channel_id=1, source_target_pairs={{0,4},{1,5},{2,6},{3,7},{4,0},{5,1},{6,2},{7,3},{8,12},{9,13},{10,... | collective-permute-start | bytes 294920 | tf_op jit(solution)/shard_map/ppermute | solution.py:36
  6.0 8.6 %collective-permute-start.2 = (bf16[64,768]{1,0:T(8,128)(2,1)S(1)}, bf16[64,768]{1,0:T(8,128)(2,1)S(1)}, u32[]{:S(2)}, u32[]{:S(2)}) collective-permute-start(bf16[64,768]{1,0:T(8,128)(2,1)S(1)} %get-tuple-element.47), channel_id=1, source_target_pairs={{0,1},{1,0},{2,4},{3,5},{4,2},{5,3},{6,8},{7,9},{8,6},{9,7},{10,12... | collective-permute-start | bytes 294920 | tf_op jit(solution)/shard_map/ppermute | solution.py:36
  7.3 7.5 %collective-permute-start.3 = (bf16[64,768]{1,0:T(8,128)(2,1)S(1)}, bf16[64,768]{1,0:T(8,128)(2,1)S(1)}, u32[]{:S(2)}, u32[]{:S(2)}) collective-permute-start(bf16[64,768]{1,0:T(8,128)(2,1)S(1)} %get-tuple-element.48), channel_id=1, source_target_pairs={{0,1},{1,0},{2,3},{3,2},{4,8},{5,9},{6,10},{7,11},{8,4},{9,5},{10,... | collective-permute-start | bytes 294920 | tf_op jit(solution)/shard_map/ppermute | solution.py:36
  8.8 6.0 %collective-permute-start.4 = (bf16[64,768]{1,0:T(8,128)(2,1)S(1)}, bf16[64,768]{1,0:T(8,128)(2,1)S(1)}, u32[]{:S(2)}, u32[]{:S(2)}) collective-permute-start(bf16[64,768]{1,0:T(8,128)(2,1)S(1)} %get-tuple-element.49), channel_id=1, source_target_pairs={{0,2},{1,3},{2,0},{3,1},{4,6},{5,7},{6,4},{7,5},{8,10},{9,11},{10,... | collective-permute-start | bytes 294920 | tf_op jit(solution)/shard_map/ppermute | solution.py:36
  14.9 1.4 %collective-permute-start.5 = (bf16[64,768]{1,0:T(8,128)(2,1)S(1)}, bf16[64,768]{1,0:T(8,128)(2,1)S(1)}, u32[]{:S(2)}, u32[]{:S(2)}) collective-permute-start(bf16[64,768]{1,0:T(8,128)(2,1)S(1)} %shard_map.151.refs_0_.piece), channel_id=1, source_target_pairs={{0,1},{1,0},{2,3},{3,2},{4,5},{5,4},{6,7},{7,6},{8,9},{9,8},{10,11... | collective-permute-start | bytes 294920 | tf_op jit(solution)/shard_map/ppermute | solution.py:18
  15.0 3.6 %copy-start.7 = (s32[1,384]{1,0:T(1,128)S(1)}, s32[1,384]{1,0:T(1,128)}, u32[]{:S(2)}) copy-start(s32[1,384]{1,0:T(1,128)} %param.20) | copy-start | bytes 4612
  15.0 3.7 %copy-start = (bf16[1,1152,576]{1,2,0:T(8,128)(2,1)S(1)}, bf16[1,1152,576]{1,2,0:T(8,128)(2,1)}, u32[]{:S(2)}) copy-start(bf16[1,1152,576]{1,2,0:T(8,128)(2,1)} %param.23) | copy-start | bytes 3981316
  15.0 3.7 %copy-start.2 = (bf16[1,1152,192]{1,2,0:T(8,128)(2,1)S(1)}, bf16[1,1152,192]{1,2,0:T(8,128)(2,1)}, u32[]{:S(2)}) copy-start(bf16[1,1152,192]{1,2,0:T(8,128)(2,1)} %param.22) | copy-start | bytes 1327108
  16.5 5.8 %collective-permute-start.6 = (bf16[64,192]{1,0:T(8,128)(2,1)S(1)}, bf16[64,192]{1,0:T(8,128)(2,1)S(1)}, u32[]{:S(2)}, u32[]{:S(2)}) collective-permute-start(bf16[64,192]{1,0:T(8,128)(2,1)S(1)} %get-tuple-element.55), channel_id=1, source_target_pairs={{0,1},{1,0},{2,4},{3,5},{4,2},{5,3},{6,8},{7,9},{8,6},{9,7},{10,12... | collective-permute-start | bytes 73736 | tf_op jit(solution)/shard_map/ppermute | solution.py:36
  18.0 4.4 %collective-permute-start.7 = (bf16[64,192]{1,0:T(8,128)(2,1)S(1)}, bf16[64,192]{1,0:T(8,128)(2,1)S(1)}, u32[]{:S(2)}, u32[]{:S(2)}) collective-permute-start(bf16[64,192]{1,0:T(8,128)(2,1)S(1)} %get-tuple-element.56), channel_id=1, source_target_pairs={{0,2},{1,3},{2,0},{3,1},{4,6},{5,7},{6,4},{7,5},{8,10},{9,11},{10,... | collective-permute-start | bytes 73736 | tf_op jit(solution)/shard_map/ppermute | solution.py:36

commit v6 on v5

--- a/solution.py
+++ b/solution.py
@@ -168,13 +168,12 @@
     refs[-1][...] = total.astype(BF16)
 
 
-def update_kernel(panel, *refs):
-    pieces, first, sends = refs[:-4], refs[-4:-2], refs[-2:]
+def update_kernel(flip, panel, begun, *refs):
+    pieces, send = refs[:-1], refs[-1]
     width = pieces[0].shape[1]
     parent = jnp.concatenate([piece[...] for piece in pieces], axis=1)
-    for begun, send, flip in zip(first, sends, (True, False)):
-        slot = jnp.where(goes_up(lax.axis_index("box"), 1, flip), 1, 0)
-        send[...] = (begun[...] + dot(parent, panel[slot, width:])).astype(BF16)
+    slot = jnp.where(goes_up(lax.axis_index("box"), 1, flip), 1, 0)
+    send[...] = (begun[...] + dot(parent, panel[slot, width:])).astype(BF16)
 
 
 def own_update_kernel(panel, piece, *sends):
@@ -270,12 +269,14 @@
         out_shape=(struct((columns, s2_block), F32),) * 2,
         compiler_params=params,
     )(panel_spread, pieces[0])
-    updates = pl.pallas_call(
-        update_kernel,
-        out_shape=(struct((columns, s2_block), BF16),) * 2,
-        compiler_params=params,
-    )(panel_spread, *pieces[1:], *begun)
-    moved = [box_permute(piece, 1, flip) for piece, flip in zip(updates, (True, False))]
+    moved = []
+    for flip, part in zip((True, False), begun):
+        update = pl.pallas_call(
+            functools.partial(update_kernel, flip),
+            out_shape=struct((columns, s2_block), BF16),
+            compiler_params=params,
+        )(panel_spread, part, *pieces[1:])
+        moved.append(box_permute(update, 1, flip))
     red_two, ys2 = pl.pallas_call(
         finish_kernel,
         out_shape=(struct((1, columns, i2_block), F32), struct((1, columns, s2_block), F32)),

time: 23.2 us -> 23.2 us (level)
  waiting for transfers between devices: 3.13 us -> 2.88 us
    ppermute x6, waiting for transfers between devices: 2.15 us -> 1.86 us  [box_permute(): return lax.ppermute(block, ('box', 'row'), route)]
  transfers between devices with their start and end apart: 8 -> 8, of which waited for: 4 -> 4; matrix products, arithmetic and copies ran while one was open for 1% -> 1% of each run, Pallas kernels for 35% -> 36%
where the time goes in v6:
time: 23.2 us; the launch traced here: 22.9 us
  Pallas kernels  10.1 us (44%)
  starting transfers between devices  8.27 us (36%)
  waiting for transfers between devices  2.88 us (12%)
  other arithmetic  0.83 us (4%)
  between operations  0.8 us (3%)
    ppermute x6, starting transfers between devices, box_permute(): return lax.ppermute(block, ('box', 'row'), route)  8.12 us
    pallas_call x1, Pallas kernels, shards(): pl.pallas_call(spread_kernel, out_shape=(struct((groups, columns, inv1.sh...  3.86 us
    pallas_call x1, Pallas kernels, shards(): pl.pallas_call(pick_kernel, out_shape=(struct((groups, columns, redundant...  1.92 us
    pallas_call x1, Pallas kernels, shards(): pl.pallas_call(finish_kernel, out_shape=(struct((1, columns, i2_block), F...  1.91 us
    ppermute x6, waiting for transfers between devices, box_permute(): return lax.ppermute(block, ('box', 'row'), route)  1.86 us
    pallas_call x1, Pallas kernels, shards(): pl.pallas_call(functools.partial(leaf_kernel, rows, block), out_shape=(st...  1.7 us
    ppermute x2, waiting for transfers between devices, row_pieces(): lax.ppermute(block, 'row', [(i, i ^ t) for i in range(rows)])  1.02 us
    add x1, other arithmetic, shards(): skel_two = ys2 + moved[0].astype(F32)[None] + moved[1].astype(F32)[None]  0.64 us
  transfers between devices with their start and end apart: 8, of which 4 were waited for; matrix products, arithmetic and copies ran while one was open for 1% of the time, Pallas kernels for 36%

profile of v6, /device:TPU:24, one launch (start us, length us, event | category | flops | bytes accessed | tf_op | source)
XLA Modules:
  0.0 22.9 jit_solution(17392336743809312228)
XLA Ops:
  0.6 0.1 collective-permute-start
  0.7 1.9 %shard_map.148 = (bf16[8,64,128]{2,1,0:T(8,128)(2,1)S(1)}, f32[8,64,320]{2,1,0:T(8,128)S(1)}, s32[8,8]{1,0:T(8,128)S(1)}, bf16[8,8,128,128]{3,2,1,0:T(8,128)(2,1)S(1)}, bf16[8,64,128]{2,1,0:T(8,128)(2,1)S(1)}) custom-call(s32[8,128]{1,0:T(8,128)} %red.1, f32[8,64,320]{2,1,0:T(8,128)} %rhs.1, s32[8,8]{1,0:T(8,128)} %near.1, bf16[8,8,96,128]{3,2,1,0:T(8,128)(2,1)} %bitcast.16, ...), custom_call_target="tpu_custom_call" | custom-call | tf_op jit(solution)/shard_map/pallas_call | solution.py:216
  2.6 0.0 copy-start.6
  2.7 0.0 copy-start.1
  2.7 0.0 copy-start.3
  2.7 0.0 copy-start.4
  2.7 0.0 copy-start.5
  2.7 0.0 collective-permute-done.refs_1_
  2.7 1.7 %shard_map.149 = (f32[64,768]{1,0:T(8,128)S(1)}, bf16[64,768]{1,0:T(8,128)(2,1)S(1)}, bf16[64,768]{1,0:T(8,128)(2,1)S(1)}, bf16[64,768]{1,0:T(8,128)(2,1)S(1)}, bf16[64,768]{1,0:T(8,128)(2,1)S(1)}) custom-call(s32[8,8]{1,0:T(8,128)S(1)} %get-tuple-element.28.near_held, bf16[8,64,128]{2,1,0:T(8,128)(2,1)S(1)} %get-tuple-element.29.xr, ...), custom_call_target="tpu_custom_call" | custom-call | tf_op jit(solution)/shard_map/pallas_call | solution.py:230
  4.4 1.6 %collective-permute-start.1 = (bf16[64,768]{1,0:T(8,128)(2,1)S(1)}, bf16[64,768]{1,0:T(8,128)(2,1)S(1)}, u32[]{:S(2)}, u32[]{:S(2)}) collective-permute-start(bf16[64,768]{1,0:T(8,128)(2,1)S(1)} %get-tuple-element.32), channel_id=1, source_target_pairs={{0,4},{1,5},{2,6},{3,7},{4,0},{5,1},{6,2},{7,3},{8,12},{9,13},{10,... | collective-permute-start | bytes 294920 | tf_op jit(solution)/shard_map/ppermute | solution.py:36
  6.0 1.3 %collective-permute-start.2 = (bf16[64,768]{1,0:T(8,128)(2,1)S(1)}, bf16[64,768]{1,0:T(8,128)(2,1)S(1)}, u32[]{:S(2)}, u32[]{:S(2)}) collective-permute-start(bf16[64,768]{1,0:T(8,128)(2,1)S(1)} %get-tuple-element.45), channel_id=1, source_target_pairs={{0,1},{1,0},{2,4},{3,5},{4,2},{5,3},{6,8},{7,9},{8,6},{9,7},{10,12... | collective-permute-start | bytes 294920 | tf_op jit(solution)/shard_map/ppermute | solution.py:36
  7.3 1.5 %collective-permute-start.3 = (bf16[64,768]{1,0:T(8,128)(2,1)S(1)}, bf16[64,768]{1,0:T(8,128)(2,1)S(1)}, u32[]{:S(2)}, u32[]{:S(2)}) collective-permute-start(bf16[64,768]{1,0:T(8,128)(2,1)S(1)} %get-tuple-element.46), channel_id=1, source_target_pairs={{0,1},{1,0},{2,3},{3,2},{4,8},{5,9},{6,10},{7,11},{8,4},{9,5},{10,... | collective-permute-start | bytes 294920 | tf_op jit(solution)/shard_map/ppermute | solution.py:36
  8.8 1.6 %collective-permute-start.4 = (bf16[64,768]{1,0:T(8,128)(2,1)S(1)}, bf16[64,768]{1,0:T(8,128)(2,1)S(1)}, u32[]{:S(2)}, u32[]{:S(2)}) collective-permute-start(bf16[64,768]{1,0:T(8,128)(2,1)S(1)} %get-tuple-element.47), channel_id=1, source_target_pairs={{0,2},{1,3},{2,0},{3,1},{4,6},{5,7},{6,4},{7,5},{8,10},{9,11},{10,... | collective-permute-start | bytes 294920 | tf_op jit(solution)/shard_map/ppermute | solution.py:36
  10.4 0.0 copy-done.6
  10.4 0.1 fusion.red
  10.5 0.0 copy-done.1
  10.5 0.0 copy-done.3
  10.5 0.0 copy-done.4
  10.5 0.0 copy-done.5
  10.5 3.9 %shard_map.150 = (f32[8,64,64]{2,1,0:T(8,128)}, f32[64,768]{1,0:T(8,128)S(1)}, bf16[2,1536,192]{2,1,0:T(8,128)(2,1)S(1)}) custom-call(s32[1,2]{1,0:T(1,128)S(1)} %copy-done.5, s32[1,1152]{1,0:T(1,128)S(1)} %fusion.red, bf16[1,2,192,1152]{3,2,1,0:T(8,128)(2,1)S(1)} %bitcast.13, bf16[8,64,128]{2,1,0:T(8,128)(2,1)S(1)} %get-tuple-element.29.xr, ...), custom_call_target="tpu_custom_call" | custom-call | tf_op jit(solution)/shard_map/pallas_call | solution.py:255
  14.4 0.0 collective-permute-done.1.refs_1_
  14.4 0.2 %collective-permute-done.2.refs_2_ = bf16[64,768]{1,0:T(8,128)(2,1)S(1)} collective-permute-done((bf16[64,768]{1,0:T(8,128)(2,1)S(1)}, bf16[64,768]{1,0:T(8,128)(2,1)S(1)}, u32[]{:S(2)}, u32[]{:S(2)}) %collective-permute-start.2) | collective-permute-done | bytes 98336 | tf_op jit(solution)/shard_map/ppermute | solution.py:36
  14.6 0.2 collective-permute-done.3.refs_3_
  14.8 0.0 collective-permute-done.4.refs_4_
  14.8 0.1 shard_map.151.refs_0_.piece
  14.9 0.1 collective-permute-start.5
  15.0 0.3 %shard_map.153 = (f32[64,192]{1,0:T(8,128)S(1)}, f32[64,192]{1,0:T(8,128)S(1)}) custom-call(bf16[2,1536,192]{2,1,0:T(8,128)(2,1)S(1)} %get-tuple-element.50.panel, bf16[64,768]{1,0:T(8,128)(2,1)S(1)} %shard_map.151.refs_0_.piece), custom_call_target="tpu_custom_call" | custom-call | tf_op jit(solution)/shard_map/pallas_call | solution.py:267
  15.2 1.0 %collective-permute-done.5.refs_1_.refs_0_ = bf16[64,768]{1,0:T(8,128)(2,1)S(1)} collective-permute-done((bf16[64,768]{1,0:T(8,128)(2,1)S(1)}, bf16[64,768]{1,0:T(8,128)(2,1)S(1)}, u32[]{:S(2)}, u32[]{:S(2)}) %collective-permute-start.5) | collective-permute-done | bytes 98336 | tf_op jit(solution)/shard_map/ppermute | solution.py:18
  16.3 0.0 copy-start.7
  16.3 0.0 copy-start
  16.3 0.0 copy-start.2
  16.3 0.2 shard_map.154
  16.5 1.5 %collective-permute-start.6 = (bf16[64,192]{1,0:T(8,128)(2,1)S(1)}, bf16[64,192]{1,0:T(8,128)(2,1)S(1)}, u32[]{:S(2)}, u32[]{:S(2)}) collective-permute-start(bf16[64,192]{1,0:T(8,128)(2,1)S(1)} %shard_map.154), channel_id=1, source_target_pairs={{0,1},{1,0},{2,4},{3,5},{4,2},{5,3},{6,8},{7,9},{8,6},{9,7},{10,12... | collective-permute-start | bytes 73736 | tf_op jit(solution)/shard_map/ppermute | solution.py:36
  17.9 0.2 shard_map.155
  18.2 0.7 %collective-permute-start.7 = (bf16[64,192]{1,0:T(8,128)(2,1)S(1)}, bf16[64,192]{1,0:T(8,128)(2,1)S(1)}, u32[]{:S(2)}, u32[]{:S(2)}) collective-permute-start(bf16[64,192]{1,0:T(8,128)(2,1)S(1)} %shard_map.155), channel_id=1, source_target_pairs={{0,2},{1,3},{2,0},{3,1},{4,6},{5,7},{6,4},{7,5},{8,10},{9,11},{10,... | collective-permute-start | bytes 73736 | tf_op jit(solution)/shard_map/ppermute | solution.py:36
  18.8 0.0 copy-done.7
  18.8 0.1 fusion.1.skel
  18.9 0.0 copy-done
  19.0 0.0 copy-done.2
  19.0 1.9 %shard_map.152 = (f32[1,64,576]{2,1,0:T(8,128)}, f32[1,64,192]{2,1,0:T(8,128)S(1)}) custom-call(s32[1,1152]{1,0:T(1,128)S(1)} %fusion.red, s32[1,192]{1,0:T(1,128)S(1)} %fusion.1.skel, bf16[1,576,1152]{2,1,0:T(8,128)(2,1)S(1)} %bitcast.12, bf16[1,192,1152]{2,1,0:T(8,128)(2,1)S(1)} %bitcast.14, bf16[64,768]{1,0:T(8,128)(2,1)S(1)} %shard_map.151.refs_0_.piece, ...), custom_call_target="tpu_custom_call" | custom-call | tf_op jit(solution)/shard_map/pallas_call | solution.py:280
  20.9 1.4 %collective-permute-done.6 = bf16[64,192]{1,0:T(8,128)(2,1)S(1)} collective-permute-done((bf16[64,192]{1,0:T(8,128)(2,1)S(1)}, bf16[64,192]{1,0:T(8,128)(2,1)S(1)}, u32[]{:S(2)}, u32[]{:S(2)}) %collective-permute-start.6) | collective-permute-done | bytes 24608 | tf_op jit(solution)/shard_map/ppermute | solution.py:36
  22.3 0.0 collective-permute-done.7
  22.3 0.6 %convert_add_fusion = f32[1,64,192]{2,1,0:T(8,128)} fusion(f32[1,64,192]{2,1,0:T(8,128)S(1)} %get-tuple-element.49, bf16[64,192]{1,0:T(8,128)(2,1)S(1)} %collective-permute-done.7, bf16[64,192]{1,0:T(8,128)(2,1)S(1)} %collective-permute-done.6), kind=kLoop, calls=%fused_computation | loop fusion | flops 49152 | bytes 147456 | tf_op jit(solution)/shard_map/add | solution.py:285
Async XLA Ops:
  0.6 2.1 %collective-permute-start = (bf16[8,64,128]{2,1,0:T(8,128)(2,1)}, bf16[8,64,128]{2,1,0:T(8,128)(2,1)S(1)}, u32[]{:S(2)}, u32[]{:S(2)}) collective-permute-start(bf16[8,64,128]{2,1,0:T(8,128)(2,1)} %bitcast.17), channel_id=1, source_target_pairs={{0,1},{1,0},{2,3},{3,2},{4,5},{5,4},{6,7},{7,6},{8,9},{9,8},{10,11... | collective-permute-start | bytes 393224 | tf_op jit(solution)/shard_map/ppermute | solution.py:18
  2.6 7.8 %copy-start.6 = (s32[1,1152]{1,0:T(1,128)S(1)}, s32[1,1152]{1,0:T(1,128)}, u32[]{:S(2)}) copy-start(s32[1,1152]{1,0:T(1,128)} %param.21) | copy-start | bytes 13828
  2.7 7.8 %copy-start.1 = (bf16[1,2,1152,192]{2,3,1,0:T(8,128)(2,1)S(1)}, bf16[1,2,1152,192]{2,3,1,0:T(8,128)(2,1)}, u32[]{:S(2)}) copy-start(bf16[1,2,1152,192]{2,3,1,0:T(8,128)(2,1)} %param.24) | copy-start | bytes 2654212
  2.7 7.8 %copy-start.3 = (bf16[8,128,96]{1,2,0:T(8,128)(2,1)S(1)}, bf16[8,128,96]{1,2,0:T(8,128)(2,1)}, u32[]{:S(2)}) copy-start(bf16[8,128,96]{1,2,0:T(8,128)(2,1)} %param.16) | copy-start | bytes 589828
  2.7 7.8 %copy-start.4 = (s32[8,192]{1,0:T(8,128)S(1)}, s32[8,192]{1,0:T(8,128)}, u32[]{:S(2)}) copy-start(s32[8,192]{1,0:T(8,128)} %skel) | copy-start | bytes 18436
  2.7 7.8 %copy-start.5 = (s32[1,2]{1,0:T(1,128)S(1)}, s32[1,2]{1,0:T(1,128)}, u32[]{:S(2)}) copy-start(s32[1,2]{1,0:T(1,128)} %near.2) | copy-start | bytes 28
  4.4 10.0 %collective-permute-start.1 = (bf16[64,768]{1,0:T(8,128)(2,1)S(1)}, bf16[64,768]{1,0:T(8,128)(2,1)S(1)}, u32[]{:S(2)}, u32[]{:S(2)}) collective-permute-start(bf16[64,768]{1,0:T(8,128)(2,1)S(1)} %get-tuple-element.32), channel_id=1, source_target_pairs={{0,4},{1,5},{2,6},{3,7},{4,0},{5,1},{6,2},{7,3},{8,12},{9,13},{10,... | collective-permute-start | bytes 294920 | tf_op jit(solution)/shard_map/ppermute | solution.py:36
  6.0 8.6 %collective-permute-start.2 = (bf16[64,768]{1,0:T(8,128)(2,1)S(1)}, bf16[64,768]{1,0:T(8,128)(2,1)S(1)}, u32[]{:S(2)}, u32[]{:S(2)}) collective-permute-start(bf16[64,768]{1,0:T(8,128)(2,1)S(1)} %get-tuple-element.45), channel_id=1, source_target_pairs={{0,1},{1,0},{2,4},{3,5},{4,2},{5,3},{6,8},{7,9},{8,6},{9,7},{10,12... | collective-permute-start | bytes 294920 | tf_op jit(solution)/shard_map/ppermute | solution.py:36
  7.3 7.5 %collective-permute-start.3 = (bf16[64,768]{1,0:T(8,128)(2,1)S(1)}, bf16[64,768]{1,0:T(8,128)(2,1)S(1)}, u32[]{:S(2)}, u32[]{:S(2)}) collective-permute-start(bf16[64,768]{1,0:T(8,128)(2,1)S(1)} %get-tuple-element.46), channel_id=1, source_target_pairs={{0,1},{1,0},{2,3},{3,2},{4,8},{5,9},{6,10},{7,11},{8,4},{9,5},{10,... | collective-permute-start | bytes 294920 | tf_op jit(solution)/shard_map/ppermute | solution.py:36
  8.8 6.0 %collective-permute-start.4 = (bf16[64,768]{1,0:T(8,128)(2,1)S(1)}, bf16[64,768]{1,0:T(8,128)(2,1)S(1)}, u32[]{:S(2)}, u32[]{:S(2)}) collective-permute-start(bf16[64,768]{1,0:T(8,128)(2,1)S(1)} %get-tuple-element.47), channel_id=1, source_target_pairs={{0,2},{1,3},{2,0},{3,1},{4,6},{5,7},{6,4},{7,5},{8,10},{9,11},{10,... | collective-permute-start | bytes 294920 | tf_op jit(solution)/shard_map/ppermute | solution.py:36
  14.9 1.4 %collective-permute-start.5 = (bf16[64,768]{1,0:T(8,128)(2,1)S(1)}, bf16[64,768]{1,0:T(8,128)(2,1)S(1)}, u32[]{:S(2)}, u32[]{:S(2)}) collective-permute-start(bf16[64,768]{1,0:T(8,128)(2,1)S(1)} %shard_map.151.refs_0_.piece), channel_id=1, source_target_pairs={{0,1},{1,0},{2,3},{3,2},{4,5},{5,4},{6,7},{7,6},{8,9},{9,8},{10,11... | collective-permute-start | bytes 294920 | tf_op jit(solution)/shard_map/ppermute | solution.py:18
  16.3 2.6 %copy-start.7 = (s32[1,384]{1,0:T(1,128)S(1)}, s32[1,384]{1,0:T(1,128)}, u32[]{:S(2)}) copy-start(s32[1,384]{1,0:T(1,128)} %param.20) | copy-start | bytes 4612
  16.3 2.7 %copy-start = (bf16[1,1152,576]{1,2,0:T(8,128)(2,1)S(1)}, bf16[1,1152,576]{1,2,0:T(8,128)(2,1)}, u32[]{:S(2)}) copy-start(bf16[1,1152,576]{1,2,0:T(8,128)(2,1)} %param.23) | copy-start | bytes 3981316
  16.3 2.7 %copy-start.2 = (bf16[1,1152,192]{1,2,0:T(8,128)(2,1)S(1)}, bf16[1,1152,192]{1,2,0:T(8,128)(2,1)}, u32[]{:S(2)}) copy-start(bf16[1,1152,192]{1,2,0:T(8,128)(2,1)} %param.22) | copy-start | bytes 1327108
  16.5 5.8 %collective-permute-start.6 = (bf16[64,192]{1,0:T(8,128)(2,1)S(1)}, bf16[64,192]{1,0:T(8,128)(2,1)S(1)}, u32[]{:S(2)}, u32[]{:S(2)}) collective-permute-start(bf16[64,192]{1,0:T(8,128)(2,1)S(1)} %shard_map.154), channel_id=1, source_target_pairs={{0,1},{1,0},{2,4},{3,5},{4,2},{5,3},{6,8},{7,9},{8,6},{9,7},{10,12... | collective-permute-start | bytes 73736 | tf_op jit(solution)/shard_map/ppermute | solution.py:36
  18.2 4.1 %collective-permute-start.7 = (bf16[64,192]{1,0:T(8,128)(2,1)S(1)}, bf16[64,192]{1,0:T(8,128)(2,1)S(1)}, u32[]{:S(2)}, u32[]{:S(2)}) collective-permute-start(bf16[64,192]{1,0:T(8,128)(2,1)S(1)} %shard_map.155), channel_id=1, source_target_pairs={{0,2},{1,3},{2,0},{3,1},{4,6},{5,7},{6,4},{7,5},{8,10},{9,11},{10,... | collective-permute-start | bytes 73736 | tf_op jit(solution)/shard_map/ppermute | solution.py:36
